TPU v7x, 768 devices: a whole 4x8x12 slice. The times are simulated.
768 devices in a mesh: band: 24 (over z, y_hi), ga: 32 (over x, y_lo, core).
Axes of the slice: x: 4, y: 8 (y_hi: 2, y_lo: 4; y = y_hi * 4 + y_lo), z: 12, core: 2. Of those that a mesh axis runs over, the one named last changes fastest.
Arguments:
- pair_dens: bfloat16 [24, 48, 36864], P('band', None, 'ga'), may hold values from -0.03125 to 0.03125
- energies: float32 [24], P('band'), may hold values from -2 to 2
- freq_index: int32 [1], replicated, may hold values from 0 to 15
- screened: bfloat16 [24, 32, 48, 36864], P('band', None, None, 'ga'), may hold values from -6 to 6
Outputs:
- sigma: float32 [48, 48], P('band')
All inputs are finite; a program needn't handle non-finite values.
Results may differ from a plain program's by a relative error of at most 0.012.
Values may be sent and summed in bfloat16 or wider, within the bound.
No kernel may reach another device: no remote copies, remote signals or barrier semaphores. Data moves between devices by JAX's collectives and lax.ppermute only.
A program may use at most 64 MiB of HBM per device.

v0:
```python
import jax
import jax.numpy as jnp
from jax import lax
from jax.sharding import PartitionSpec as P

NFREQ = 16


def on_device(pair_dens, energies, freq_index, screened):
    band_count = lax.axis_size("band")
    band_pos = lax.axis_index("band")
    subrows = pair_dens.shape[2] // band_count
    slab_all, energy_all = (
        lax.all_gather(pair_dens, "band", axis=0, tiled=True),
        lax.all_gather(energies.astype(jnp.bfloat16), "band", axis=0, tiled=True).astype(
            energies.dtype
        ),
    )
    piece = lax.dynamic_slice_in_dim(slab_all, band_pos * subrows, subrows, 2)
    row_block = lax.all_gather(piece, "ga", axis=2, tiled=True)
    mcount, nbands, rowcount = row_block.shape
    panel = screened.reshape(rowcount, screened.shape[3])
    proj = jnp.dot(
        row_block.reshape(mcount * nbands, rowcount), panel, preferred_element_type=jnp.float32
    )
    proj = proj.reshape(mcount, nbands, panel.shape[1])
    omega = 0.1 * jnp.exp(jnp.log(20.0) * freq_index[0].astype(jnp.float32) / (NFREQ - 1))
    coef = energy_all / (energy_all * energy_all + omega * omega)
    weighted = (proj * coef[:, None, None]).astype(jnp.bfloat16)
    partial_sigma = jnp.einsum(
        "mng,mpg->np", weighted, slab_all, preferred_element_type=jnp.float32
    )
    total = lax.psum(partial_sigma, ("band", "ga"))
    row_share = nbands // band_count
    return lax.dynamic_slice_in_dim(total, band_pos * row_share, row_share, 0)


def solution(mesh):
    return jax.shard_map(
        on_device,
        mesh=mesh,
        in_specs=(P("band", None, "ga"), P("band"), P(), P("band", None, None, "ga")),
        out_specs=P("band", None),
        check_vma=False,
    )
```

profile of v0, /device:TPU:1, one launch (start us, length us, event | category | flops | bytes accessed | tf_op | source)
XLA Modules:
  0.0 368.9 jit_solution(15866096691126218155)
XLA Ops:
  6.5 0.0 copy-start
  6.5 0.0 all-gather.3.cloned.1.call-start
  6.5 0.7 all-gather.3.cloned.1.call-update
  7.3 0.0 all-gather.5.cloned.1.call-start
  7.3 145.2 %all-gather.3.cloned.1.call-done = bf16[24,48,1152]{2,1,0:T(8,128)(2,1)} async-done(((bf16[1,48,1152]{2,1,0:T(8,128)(2,1)}), bf16[24,48,1152]{2,1,0:T(8,128)(2,1)}) %all-gather.3.cloned.1.call-update) | async-done | bytes 2654224 | tf_op jit(solution)/shard_map/all_gather | solution.py:14
  152.5 1.9 constant_dynamic-slice_fusion.1
  154.4 1.8 copy.5
  156.2 0.0 all-gather.5.cloned.1.call-update
  156.9 1.3 dynamic-slice
  158.2 0.8 dynamic-update-slice
  159.0 59.2 %all-reduce = bf16[24]{0:T(256)(128)(2,1)S(1)} all-reduce(bf16[24]{0:T(256)(128)(2,1)S(1)} %dynamic-update-slice), channel_id=1, replica_groups=mesh['band'=24,'ga'=32] {'band'}, use_global_device_ids=true, to_apply=%add | all-reduce | flops 24 | bytes 96
  218.8 19.9 %all-gather.5.cloned.1.call-done = bf16[24,48,1536]{1,0,2:T(8,128)(2,1)} async-done(((bf16[24,48,48]{1,0,2:T(8,128)(2,1)}), bf16[24,48,1536]{1,0,2:T(8,128)(2,1)}) %all-gather.5.cloned.1.call-update) | async-done | bytes 3538960 | tf_op jit(solution)/shard_map/all_gather | solution.py:20
  238.7 0.0 copy-done
  238.7 11.7 %fusion.7 = f32[48,48]{1,0:T(8,128)} fusion(bf16[24,48,1152]{2,1,0:T(8,128)(2,1)} %all-gather.3.cloned.1.call-done, bf16[1536,1152,1]{1,0,2:T(8,128)(2,1)S(1)} %bitcast.9, bf16[24,48,1536]{1,0,2:T(8,128)(2,1)} %all-gather.5.cloned.1.call-done, f32[24]{0:T(128)S(1)} %add_divide_fusion), kind=kOutput, calls=%fused_computation.4 | convolution fusion | flops 4206919680 | bytes 9741408 | tf_op jit(solution)/shard_map/mng,mpg->np/dot_general | solution.py:30
  250.5 110.4 %psum.7 = f32[48,48]{1,0:T(8,128)} all-reduce(f32[48,48]{1,0:T(8,128)} %fusion.7), channel_id=1, replica_groups=mesh['band'=24,'ga'=32] {'band','ga'}, use_global_device_ids=true, to_apply=%region_0.0 | all-reduce | flops 2304 | bytes 18432 | tf_op jit(solution)/shard_map/psum | solution.py:33
  360.8 1.2 constant_dynamic-slice_fusion
  (2 shorter events, 0.0 us)
Async XLA Ops:
  6.5 232.2 %copy-start = (bf16[1,32,48,1152]{3,2,1,0:T(8,128)(2,1)S(1)}, bf16[1,32,48,1152]{3,2,1,0:T(8,128)(2,1)}, u32[]{:S(2)}) copy-start(bf16[1,32,48,1152]{3,2,1,0:T(8,128)(2,1)} %param.7) | copy-start | bytes 10616836
  6.5 145.9 %all-gather.3.cloned.1.call-start = ((), (), s32[]{:S(2)}) async-start(), calls=%async_computation | async-start | bytes 2764800 | tf_op jit(solution)/shard_map/all_gather | solution.py:14
  7.3 231.5 %all-gather.5.cloned.1.call-start = ((), (), s32[]{:S(2)}) async-start(), calls=%async_computation.1 | async-start | bytes 9732096 | tf_op jit(solution)/shard_map/all_gather | solution.py:20
Sparse Core Ops, SparseCore 0:
  10.9 141.4 all-gather.2
  156.4 82.3 all-gather.4
where the time goes:
time: 369 us
  blocking collectives  170 us (46%)
  waiting for transfers between devices  166 us (45%)
  between operations  14.8 us (4%)
  matrix products  11.7 us (3%)
  local copies, waits for them, and re-layouts  7.04 us (2%)
    all_gather x1, waiting for transfers between devices, on_device(): lax.all_gather(pair_dens, 'band', axis=0, tiled=True)  145 us
    psum x1, blocking collectives, on_device(): total = lax.psum(partial_sigma, ('band', 'ga'))  110 us
    unnamed x1, blocking collectives  59.2 us
    all_gather x1, waiting for transfers between devices, on_device(): row_block = lax.all_gather(piece, 'ga', axis=2, tiled=True)  19.9 us
    dot_general x1, matrix products, on_device(): jnp.einsum('mng,mpg->np', weighted, slab_all, preferred_element_type=jnp....  11.7 us
  transfers between devices with their start and end apart: 2, of which 2 were waited for; matrix products, arithmetic and copies ran while one was open for 1% of the time, Pallas kernels for 0%

commit v1 on v0

v1 whole, which is shorter than its diff:
```python
import jax
import jax.numpy as jnp
from jax import lax
from jax.experimental import pallas as pl
from jax.experimental.pallas import tpu as pltpu
from jax.sharding import Mesh
from jax.sharding import PartitionSpec as P

NFREQ = 16
Z, YH, X, YL, CORE = 12, 2, 4, 4, 2
BAND = ("z", "yh")
GA = ("x", "yl", "core")
GROUP = 8


def turn_kernel(core_ref, w_ref, out_ref):
    core = core_ref[0]
    half = out_ref.shape[1] // 2
    for side in range(2):
        owner = jnp.where(side == 0, core, 1 - core)
        rows = jnp.concatenate([w_ref[2 * i + owner] for i in range(X * YL)], axis=0)
        out_ref[:, side * half : (side + 1) * half] = rows.T


def proj_kernel(wt_ref, own_ref, other_ref, out_ref):
    half = own_ref.shape[0]
    total = jnp.dot(wt_ref[:, :half], own_ref[...], preferred_element_type=jnp.float32)
    total += jnp.dot(wt_ref[:, half:], other_ref[...], preferred_element_type=jnp.float32)
    out_ref[...] = total.astype(out_ref.dtype)


def sigma_kernel(cols_ref, proj_ref, out_ref):
    nb = out_ref.shape[0]
    width = GROUP * nb
    total = jnp.zeros((nb, nb), jnp.float32)
    for g in range(cols_ref.shape[0] // width):
        block = jnp.dot(
            cols_ref[g * width : (g + 1) * width, :],
            proj_ref[:, g * width : (g + 1) * width],
            preferred_element_type=jnp.float32,
        )
        for i in range(GROUP):
            total += block[i * nb : (i + 1) * nb, i * nb : (i + 1) * nb]
    out_ref[...] = total.T


def on_device(pair_dens, energies, freq_index, screened):
    mine = pair_dens[0]
    nb, width = mine.shape
    sub = width // (Z * YH)
    rowcount = X * YL * CORE * sub

    swapped = lax.ppermute(mine, "yh", [(0, 1), (1, 0)])
    first = lax.axis_index("yh") == 0
    both = jnp.stack([jnp.where(first, mine, swapped), jnp.where(first, swapped, mine)])
    cols = lax.all_gather(both, "z").reshape(Z * YH * nb, width)

    omega = 0.1 * jnp.exp(jnp.log(20.0) * freq_index[0].astype(jnp.float32) / (NFREQ - 1))
    coef = energies[0] / (energies[0] * energies[0] + omega * omega)
    scaled = (mine.astype(jnp.float32) * coef).astype(jnp.bfloat16)
    pieces = scaled.T.reshape(Z * YH, sub, nb)
    got = lax.all_to_all(pieces, BAND, 0, 0, tiled=True)
    rows = got.transpose(1, 0, 2).reshape(sub, Z * YH * nb)
    rows = lax.all_gather(rows, "yl", axis=0, tiled=True)
    rows = lax.all_gather(rows, "x", axis=0, tiled=True)
    other = lax.ppermute(rows, "core", [(0, 1), (1, 0)])

    core = lax.axis_index("core").astype(jnp.int32).reshape(1)
    turned = pl.pallas_call(
        turn_kernel,
        out_shape=jax.ShapeDtypeStruct((width, rowcount), jnp.bfloat16),
        in_specs=[pl.BlockSpec(memory_space=pltpu.SMEM), pl.BlockSpec(memory_space=pltpu.VMEM)],
        out_specs=pl.BlockSpec(memory_space=pltpu.VMEM),
        compiler_params=pltpu.CompilerParams(vmem_limit_bytes=40 << 20),
        cost_estimate=pl.CostEstimate(flops=0, bytes_accessed=4 * rowcount * width, transcendentals=0),
    )(core, screened[0])

    mcols = Z * YH * nb
    tile = GROUP * nb
    proj = pl.pallas_call(
        proj_kernel,
        grid=(mcols // tile,),
        out_shape=jax.ShapeDtypeStruct((width, mcols), jnp.bfloat16),
        in_specs=[
            pl.BlockSpec((width, rowcount), lambda j: (0, 0)),
            pl.BlockSpec((rowcount // 2, tile), lambda j: (0, j)),
            pl.BlockSpec((rowcount // 2, tile), lambda j: (0, j)),
        ],
        out_specs=pl.BlockSpec((width, tile), lambda j: (0, j)),
        compiler_params=pltpu.CompilerParams(vmem_limit_bytes=40 << 20),
        cost_estimate=pl.CostEstimate(
            flops=2 * width * mcols * rowcount, bytes_accessed=10 << 20, transcendentals=0
        ),
    )(turned, rows, other)

    part = pl.pallas_call(
        sigma_kernel,
        out_shape=jax.ShapeDtypeStruct((nb, nb), jnp.float32),
        in_specs=[pl.BlockSpec(memory_space=pltpu.VMEM)] * 2,
        out_specs=pl.BlockSpec(memory_space=pltpu.VMEM),
        compiler_params=pltpu.CompilerParams(vmem_limit_bytes=40 << 20),
        cost_estimate=pl.CostEstimate(
            flops=2 * width * mcols * tile, bytes_accessed=6 << 20, transcendentals=0
        ),
    )(cols, proj)

    share = nb // (Z * YH)
    part = lax.all_to_all(part.reshape(Z * YH, share, nb), BAND, 0, 0, tiled=True).sum(axis=0)
    spread = jnp.broadcast_to(part[None], (X * YL * CORE, share, nb))
    return lax.all_to_all(spread, GA, 0, 0, tiled=True).sum(axis=0)


def solution(mesh):
    fine = Mesh(mesh.devices.reshape(Z, YH, X, YL, CORE), BAND + GA)
    return jax.shard_map(
        on_device,
        mesh=fine,
        in_specs=(P(BAND, None, GA), P(BAND), P(), P(BAND, None, None, GA)),
        out_specs=P(BAND, None),
        check_vma=False,
    )
```

time: 369 us -> 215 us (0.58)
  waiting for transfers between devices: 166 us -> 75.2 us
  blocking collectives: 170 us -> 93.1 us
  matrix products: 11.7 us -> 0 us
  Pallas kernels: 0 us -> 10.2 us
  starting transfers between devices: 0.04 us -> 5.7 us
  local copies, waits for them, and re-layouts: 7.04 us -> 11.1 us
  other arithmetic: 0.01 us -> 3.9 us
    psum x1 -> x0, blocking collectives: 110 us -> none  [on_device(): total = lax.psum(partial_sigma, ('band', 'ga'))]
    all_gather x2, waiting for transfers between devices: 165 us -> 65.4 us  [the longest x1 45.9 us: on_device(): cols = lax.all_gather(both, 'z').reshape(Z * YH * nb, width)]
    all_to_all x0 -> x3, blocking collectives: none -> 79.1 us  [the longest x1 35 us: on_device(): got = lax.all_to_all(pieces, BAND, 0, 0, tiled=True)]
    unnamed x1 -> x0, blocking collectives: 59.2 us -> none
    all_gather x0 -> x1, blocking collectives: none -> 14 us  [on_device(): rows = lax.all_gather(rows, 'yl', axis=0, tiled=True)]
    dot_general x1 -> x0, matrix products: 11.7 us -> none  [on_device(): jnp.einsum('mng,mpg->np', weighted, slab_all, preferred_element_type=jnp....]
    pallas_call x0 -> x3, Pallas kernels: none -> 10.2 us  [the longest x1 7.46 us: on_device(): pl.pallas_call(proj_kernel, grid=(mcols // tile,), out_shape=jax.ShapeDty...]
    ppermute x0 -> x2, waiting for transfers between devices: none -> 9.82 us  [the longest x1 7.19 us: on_device(): swapped = lax.ppermute(mine, 'yh', [(0, 1), (1, 0)])]
  transfers between devices with their start and end apart: 2 -> 4, of which waited for: 2 -> 4; matrix products, arithmetic and copies ran while one was open for 1% -> 1% of each run, Pallas kernels for 0% -> 4%
where the time goes in v1:
time: 215 us; the launch traced here: 214 us
  blocking collectives  93.1 us (43%)
  waiting for transfers between devices  75.2 us (35%)
  between operations  15.2 us (7%)
  local copies, waits for them, and re-layouts  11.1 us (5%)
  Pallas kernels  10.2 us (5%)
  starting transfers between devices  5.7 us (3%)
  other arithmetic  3.9 us (2%)
    all_gather x1, waiting for transfers between devices, on_device(): cols = lax.all_gather(both, 'z').reshape(Z * YH * nb, width)  45.9 us
    all_to_all x1, blocking collectives, on_device(): got = lax.all_to_all(pieces, BAND, 0, 0, tiled=True)  35 us
    all_to_all x1, blocking collectives, on_device(): lax.all_to_all(part.reshape(Z * YH, share, nb), BAND, 0, 0, tiled=True)  24.2 us
    all_to_all x1, blocking collectives, on_device(): return lax.all_to_all(spread, GA, 0, 0, tiled=True).sum(axis=0)  19.9 us
    all_gather x1, waiting for transfers between devices, on_device(): rows = lax.all_gather(rows, 'x', axis=0, tiled=True)  19.4 us
    all_gather x1, blocking collectives, on_device(): rows = lax.all_gather(rows, 'yl', axis=0, tiled=True)  14 us
    pallas_call x1, Pallas kernels, on_device(): pl.pallas_call(proj_kernel, grid=(mcols // tile,), out_shape=jax.ShapeDty...  7.46 us
    ppermute x1, waiting for transfers between devices, on_device(): swapped = lax.ppermute(mine, 'yh', [(0, 1), (1, 0)])  7.19 us
  transfers between devices with their start and end apart: 4, of which 4 were waited for; matrix products, arithmetic and copies ran while one was open for 1% of the time, Pallas kernels for 4%

profile of v1, /device:TPU:1, one launch (start us, length us, event | category | flops | bytes accessed | tf_op | source)
XLA Modules:
  0.0 214.3 jit_solution(9895106452827996726)
XLA Ops:
  6.5 0.0 copy-start
  6.5 0.0 all-gather.4.cloned.1.call-start
  8.2 1.6 fusion
  9.8 1.8 copy.13
  11.6 2.0 reshape.30
  13.6 35.0 %all_to_all.15 = bf16[24,2,1152]{2,1,0:T(2,128)(2,1)} all-to-all(bf16[24,2,1152]{2,1,0:T(2,128)(2,1)} %reshape.30), channel_id=1, replica_groups=mesh['z'=12,'yh'=2,'x'=4,'yl'=4,'core'=2] {'z','yh'}, dimensions={0} | all-to-all | bytes 221184 | tf_op jit(solution)/shard_map/all_to_all | solution.py:62
  48.6 1.9 reshape.31
  50.5 1.8 copy.11
  52.2 1.9 reshape.24
  54.1 14.0 %all_gather.14 = bf16[192,1152]{1,0:T(8,128)(2,1)} all-gather(bf16[48,1152]{1,0:T(8,128)(2,1)} %reshape.24), channel_id=1, replica_groups=mesh['z'=12,'yh'=2,'x'=4,'yl'=4,'core'=2] {'yl'}, dimensions={0}, use_global_device_ids=true | all-gather | bytes 552960 | tf_op jit(solution)/shard_map/all_gather | solution.py:64
  68.1 0.0 all-gather.4.cloned.1.call-update
  68.1 0.0 all-gather.6.cloned.1.call-start
  68.1 3.1 %collective-permute-start = (bf16[48,1152]{1,0:T(8,128)(2,1)}, bf16[48,1152]{1,0:T(8,128)(2,1)}, u32[]{:S(2)}, u32[]{:S(2)}) collective-permute-start(bf16[48,1152]{1,0:T(8,128)(2,1)} %bitcast.26), channel_id=1, source_target_pairs={{0,32},{32,0},{1,33},{33,1},{2,34},{34,2},{3,35},{35,3},{4,36},{36... | collective-permute-start | bytes 331784 | tf_op jit(solution)/shard_map/ppermute | solution.py:53
  71.2 7.2 %collective-permute-done = bf16[48,1152]{1,0:T(8,128)(2,1)} collective-permute-done((bf16[48,1152]{1,0:T(8,128)(2,1)}, bf16[48,1152]{1,0:T(8,128)(2,1)}, u32[]{:S(2)}, u32[]{:S(2)}) %collective-permute-start) | collective-permute-done | bytes 110624 | tf_op jit(solution)/shard_map/ppermute | solution.py:53
  78.4 1.0 select_bitcast_fusion.1
  79.4 0.7 pad_maximum_fusion
  80.1 0.0 all-gather.6.cloned.1.call-update
  80.2 19.4 %all-gather.4.cloned.1.call-done.own_ref = bf16[768,1152]{1,0:T(8,128)(2,1)} async-done(((bf16[192,1152]{1,0:T(8,128)(2,1)}), bf16[768,1152]{1,0:T(8,128)(2,1)}) %all-gather.4.cloned.1.call-update) | async-done | bytes 1769488 | tf_op jit(solution)/shard_map/all_gather | solution.py:65
  99.6 2.6 %collective-permute-start.1 = (bf16[768,1152]{1,0:T(8,128)(2,1)}, bf16[768,1152]{1,0:T(8,128)(2,1)}, u32[]{:S(2)}, u32[]{:S(2)}) collective-permute-start(bf16[768,1152]{1,0:T(8,128)(2,1)} %all-gather.4.cloned.1.call-done.own_ref), channel_id=1, source_target_pairs={{0,1},{1,0},{2,3},{3,2},{4,5},{5,4},{6,7},{7,6},{8,9},{9,8},{10,11... | collective-permute-start | bytes 5308424 | tf_op jit(solution)/shard_map/ppermute | solution.py:66
  102.2 0.0 copy-done
  102.2 0.0 copy-start.2
  102.2 1.0 shard_map.46.wt_ref
  103.2 2.6 %collective-permute-done.1.other_ref = bf16[768,1152]{1,0:T(8,128)(2,1)} collective-permute-done((bf16[768,1152]{1,0:T(8,128)(2,1)}, bf16[768,1152]{1,0:T(8,128)(2,1)}, u32[]{:S(2)}, u32[]{:S(2)}) %collective-permute-start.1) | collective-permute-done | bytes 1769504 | tf_op jit(solution)/shard_map/ppermute | solution.py:66
  105.8 0.0 copy-done.2
  105.8 7.5 %shard_map.47.proj_ref = bf16[1152,1152]{1,0:T(8,128)(2,1)S(1)} custom-call(bf16[1152,1536]{1,0:T(8,128)(2,1)S(1)} %shard_map.46.wt_ref, bf16[768,1152]{1,0:T(8,128)(2,1)S(1)} %copy-done.2, bf16[768,1152]{1,0:T(8,128)(2,1)} %collective-permute-done.1.other_ref), custom_call_target="tpu_custom_call" | custom-call | flops 4076863488 | bytes 10485760 | tf_op jit(solution)/shard_map/pallas_call | solution.py:80
  113.3 45.9 %all-gather.6.cloned.1.call-done = bf16[24,48,1152]{2,1,0:T(8,128)(2,1)} async-done(((bf16[2,48,1152]{2,1,0:T(8,128)(2,1)}), bf16[24,48,1152]{2,1,0:T(8,128)(2,1)}) %all-gather.6.cloned.1.call-update) | async-done | bytes 2654224 | tf_op jit(solution)/shard_map/all_gather | solution.py:56
  159.2 0.0 copy-start.1
  159.2 1.7 copy-done.1
  161.0 1.8 shard_map.48
  162.7 24.2 %all_to_all.16 = f32[24,2,48]{2,1,0:T(2,128)S(1)} all-to-all(f32[24,2,48]{2,1,0:T(2,128)S(1)} %bitcast.23), channel_id=1, replica_groups=mesh['z'=12,'yh'=2,'x'=4,'yl'=4,'core'=2] {'z','yh'}, dimensions={0} | all-to-all | bytes 18432 | tf_op jit(solution)/shard_map/all_to_all | solution.py:108
  187.0 19.9 %all_to_all.17 = f32[32,2,48]{2,1,0:T(2,128)S(1)} all-to-all(f32[32,2,48]{2,1,0:T(2,128)S(1)} %broadcast_in_dim.2), channel_id=1, replica_groups=mesh['z'=12,'yh'=2,'x'=4,'yl'=4,'core'=2] {'x','yl','core'}, dimensions={0} | all-to-all | bytes 24576 | tf_op jit(solution)/shard_map/all_to_all | solution.py:110
  206.9 0.6 reduce_sum.19
  (2 shorter events, 0.0 us)
Async XLA Ops:
  6.5 95.7 %copy-start = (bf16[1,32,48,1152]{3,2,1,0:T(8,128)(2,1)S(1)}, bf16[1,32,48,1152]{3,2,1,0:T(8,128)(2,1)}, u32[]{:S(2)}) copy-start(bf16[1,32,48,1152]{3,2,1,0:T(8,128)(2,1)} %param.7) | copy-start | bytes 10616836
  6.5 93.1 %all-gather.4.cloned.1.call-start = ((), (), s32[]{:S(2)}) async-start(), calls=%async_computation.3 | async-start | bytes 2211840 | tf_op jit(solution)/shard_map/all_gather | solution.py:65
  68.1 91.1 %all-gather.6.cloned.1.call-start = ((), (), s32[]{:S(2)}) async-start(), calls=%async_computation.4 | async-start | bytes 2875392 | tf_op jit(solution)/shard_map/all_gather | solution.py:56
  68.1 10.3 %collective-permute-start = (bf16[48,1152]{1,0:T(8,128)(2,1)}, bf16[48,1152]{1,0:T(8,128)(2,1)}, u32[]{:S(2)}, u32[]{:S(2)}) collective-permute-start(bf16[48,1152]{1,0:T(8,128)(2,1)} %bitcast.26), channel_id=1, source_target_pairs={{0,32},{32,0},{1,33},{33,1},{2,34},{34,2},{3,35},{35,3},{4,36},{36... | collective-permute-start | bytes 331784 | tf_op jit(solution)/shard_map/ppermute | solution.py:53
  99.6 6.2 %collective-permute-start.1 = (bf16[768,1152]{1,0:T(8,128)(2,1)}, bf16[768,1152]{1,0:T(8,128)(2,1)}, u32[]{:S(2)}, u32[]{:S(2)}) collective-permute-start(bf16[768,1152]{1,0:T(8,128)(2,1)} %all-gather.4.cloned.1.call-done.own_ref), channel_id=1, source_target_pairs={{0,1},{1,0},{2,3},{3,2},{4,5},{5,4},{6,7},{7,6},{8,9},{9,8},{10,11... | collective-permute-start | bytes 5308424 | tf_op jit(solution)/shard_map/ppermute | solution.py:66
  102.2 3.6 %copy-start.2 = (bf16[768,1152]{1,0:T(8,128)(2,1)S(1)}, bf16[768,1152]{1,0:T(8,128)(2,1)}, u32[]{:S(2)}) copy-start(bf16[768,1152]{1,0:T(8,128)(2,1)} %all-gather.4.cloned.1.call-done.own_ref) | copy-start | bytes 5308420
  159.2 1.7 copy-start.1
Sparse Core Ops, SparseCore 0:
  68.2 31.3 all-gather.3
  102.0 57.1 all-gather.5

commit v2 on v1

v2 whole, which is shorter than its diff:
```python
import jax
import jax.numpy as jnp
from jax import lax
from jax.experimental import pallas as pl
from jax.experimental.pallas import tpu as pltpu
from jax.sharding import Mesh
from jax.sharding import PartitionSpec as P

NFREQ = 16
Z, YH, X, YL, CORE = 12, 2, 4, 4, 2
BAND = ("z", "yh")
GA = ("x", "yl", "core")
GROUP = 8
VMEM = pl.BlockSpec(memory_space=pltpu.VMEM)
SMEM = pl.BlockSpec(memory_space=pltpu.SMEM)
PARAMS = pltpu.CompilerParams(vmem_limit_bytes=40 << 20)


def order_kernel(pos_ref, w_ref, out_ref):
    sub = w_ref.shape[1]
    row = 0
    for step in range(X):
        x = lax.rem(pos_ref[0] + step, X)
        for side in range(CORE):
            core = pos_ref[1] if side == 0 else 1 - pos_ref[1]
            for yl in range(YL):
                out_ref[row : row + sub, :] = w_ref[(x * YL + yl) * CORE + core]
                row += sub


def pieces_kernel(pos_ref, coef_ref, both_ref, out_ref, turned_ref):
    scaled = [both_ref[i].astype(jnp.float32) * coef_ref[i] for i in range(YH)]
    turned_ref[...] = jnp.concatenate(scaled, axis=0).T.astype(turned_ref.dtype)
    sub = out_ref.shape[1]
    for z in range(Z):
        start = pl.multiple_of((z * YH + pos_ref[0]) * sub, sub)
        out_ref[z] = turned_ref[pl.ds(start, sub), :]


def rows_kernel(got_ref, out_ref):
    out_ref[...] = jnp.concatenate([got_ref[z] for z in range(Z)], axis=1)


def half_kernel(cols_ref, w_ref, out_ref):
    out_ref[...] = lax.dot_general(
        cols_ref[...], w_ref[...], (((1,), (1,)), ((), ())), preferred_element_type=jnp.float32
    ).astype(out_ref.dtype)


def sigma_kernel(half_ref, *refs):
    row_refs, out_ref = refs[:-1], refs[-1]
    nb = out_ref.shape[0]
    width = GROUP * nb
    depth = CORE * row_refs[0].shape[0]
    total = jnp.zeros((nb, nb), jnp.float32)
    for g in range(half_ref.shape[0] // width):
        span = slice(g * width, (g + 1) * width)
        block = jnp.zeros((width, width), jnp.float32)
        for step in range(X):
            rows = jnp.concatenate([r[:, span] for r in row_refs[CORE * step : CORE * step + CORE]], axis=0)
            block += jnp.dot(
                half_ref[span, step * depth : (step + 1) * depth],
                rows,
                preferred_element_type=jnp.float32,
            )
        for i in range(GROUP):
            total += block[i * nb : (i + 1) * nb, i * nb : (i + 1) * nb]
    out_ref[...] = total.T


def on_device(pair_dens, energies, freq_index, screened):
    mine = pair_dens[0]
    nb, width = mine.shape
    sub = width // (Z * YH)
    rowcount = X * YL * CORE * sub
    mcols = Z * YH * nb
    tile = GROUP * nb
    place = {axis: lax.axis_index(axis).astype(jnp.int32) for axis in ("yh", "x", "core")}
    swap = [(0, 1), (1, 0)]

    omega = 0.1 * jnp.exp(jnp.log(20.0) * freq_index[0].astype(jnp.float32) / (NFREQ - 1))
    coef = energies / (energies * energies + omega * omega)

    theirs = lax.ppermute(mine, "yh", swap)
    their_coef = lax.ppermute(coef, "yh", swap)
    both, their_coef = lax.optimization_barrier((jnp.stack([mine, theirs]), their_coef))
    cols = lax.all_gather(both, "z").reshape(mcols, width)

    ordered = pl.pallas_call(
        order_kernel,
        out_shape=jax.ShapeDtypeStruct((rowcount, width), jnp.bfloat16),
        in_specs=[SMEM, VMEM],
        out_specs=VMEM,
        compiler_params=PARAMS,
        cost_estimate=pl.CostEstimate(flops=0, bytes_accessed=4 * rowcount * width, transcendentals=0),
    )(jnp.stack([place["x"], place["core"]]), screened[0])

    pieces = pl.pallas_call(
        pieces_kernel,
        out_shape=jax.ShapeDtypeStruct((Z, sub, YH * nb), jnp.bfloat16),
        in_specs=[SMEM, SMEM, VMEM],
        out_specs=VMEM,
        scratch_shapes=[pltpu.VMEM((width, YH * nb), jnp.bfloat16)],
        compiler_params=PARAMS,
    )(place["yh"].reshape(1), jnp.concatenate([coef, their_coef]), both)
    got = lax.all_to_all(pieces, "z", 0, 0, tiled=True)
    rows = pl.pallas_call(
        rows_kernel,
        out_shape=jax.ShapeDtypeStruct((sub, mcols), jnp.bfloat16),
        in_specs=[VMEM],
        out_specs=VMEM,
        compiler_params=PARAMS,
    )(got)
    rows = lax.all_gather(rows, "yl", axis=0, tiled=True)
    blocks = []
    for step in range(X):
        block = rows if step == 0 else lax.ppermute(rows, "x", [(i, (i - step) % X) for i in range(X)])
        blocks += [block, lax.ppermute(block, "core", swap)]

    half = pl.pallas_call(
        half_kernel,
        grid=(rowcount // tile,),
        out_shape=jax.ShapeDtypeStruct((mcols, rowcount), jnp.bfloat16),
        in_specs=[
            pl.BlockSpec((mcols, width), lambda j: (0, 0)),
            pl.BlockSpec((tile, width), lambda j: (j, 0)),
        ],
        out_specs=pl.BlockSpec((mcols, tile), lambda j: (0, j)),
        compiler_params=PARAMS,
        cost_estimate=pl.CostEstimate(
            flops=2 * width * mcols * rowcount, bytes_accessed=10 << 20, transcendentals=0
        ),
    )(cols, ordered)
    part = pl.pallas_call(
        sigma_kernel,
        out_shape=jax.ShapeDtypeStruct((nb, nb), jnp.float32),
        in_specs=[VMEM] * (1 + len(blocks)),
        out_specs=VMEM,
        compiler_params=PARAMS,
        cost_estimate=pl.CostEstimate(
            flops=2 * rowcount * mcols * tile, bytes_accessed=6 << 20, transcendentals=0
        ),
    )(half, *blocks)

    share = nb // (Z * YH)
    part = lax.all_to_all(part.reshape(Z * YH, share, nb), BAND, 0, 0, tiled=True).sum(axis=0)
    spread = jnp.broadcast_to(part[None], (X * YL * CORE, share, nb))
    return lax.all_to_all(spread, GA, 0, 0, tiled=True).sum(axis=0)


def solution(mesh):
    fine = Mesh(mesh.devices.reshape(Z, YH, X, YL, CORE), BAND + GA)
    return jax.shard_map(
        on_device,
        mesh=fine,
        in_specs=(P(BAND, None, GA), P(BAND), P(), P(BAND, None, None, GA)),
        out_specs=P(BAND, None),
        check_vma=False,
    )
```

time: 215 us -> 154 us (0.72)
  waiting for transfers between devices: 75.2 us -> 3.95 us
  starting transfers between devices: 5.7 us -> 42.9 us
  blocking collectives: 93.1 us -> 71.5 us
  local copies, waits for them, and re-layouts: 11.1 us -> 4.69 us
  Pallas kernels: 10.2 us -> 12.9 us
    all_gather x2 -> x1, waiting for transfers between devices: 65.4 us -> 0.02 us  [on_device(): cols = lax.all_gather(both, 'z').reshape(mcols, width)]
    ppermute x2 -> x9, starting transfers between devices: 5.66 us -> 42.9 us  [the longest x4 22.7 us: on_device(): blocks += [block, lax.ppermute(block, 'core', swap)]]
    all_to_all x1, blocking collectives: 35 us -> 25.5 us  [on_device(): got = lax.all_to_all(pieces, 'z', 0, 0, tiled=True)]
    all_to_all x1, blocking collectives: 24.2 us -> 17.4 us  [on_device(): lax.all_to_all(part.reshape(Z * YH, share, nb), BAND, 0, 0, tiled=True)]
    ppermute x2 -> x9, waiting for transfers between devices: 9.82 us -> 3.91 us  [the longest x1 3.89 us: on_device(): their_coef = lax.ppermute(coef, 'yh', swap)]
    all_to_all x1, blocking collectives: 19.9 us -> 14.7 us  [on_device(): return lax.all_to_all(spread, GA, 0, 0, tiled=True).sum(axis=0)]
    reshape x2 -> x0, local copies, waits for them, and re-layouts: 3.64 us -> none  [the longest x1 1.87 us: on_device(): rows = got.transpose(1, 0, 2).reshape(sub, Z * YH * nb)]
    pallas_call x1, Pallas kernels: 1.75 us -> 4.39 us  [on_device(): pl.pallas_call(sigma_kernel, out_shape=jax.ShapeDtypeStruct((nb, nb), jnp...]
  transfers between devices with their start and end apart: 4 -> 10, of which waited for: 4 -> 1; matrix products, arithmetic and copies ran while one was open for 1% -> 2% of each run, Pallas kernels for 4% -> 6%
where the time goes in v2:
time: 154 us
  blocking collectives  71.5 us (46%)
  starting transfers between devices  42.9 us (28%)
  between operations  14.9 us (10%)
  Pallas kernels  12.9 us (8%)
  local copies, waits for them, and re-layouts  4.69 us (3%)
  waiting for transfers between devices  3.95 us (3%)
  other arithmetic  2.98 us (2%)
    all_to_all x1, blocking collectives, on_device(): got = lax.all_to_all(pieces, 'z', 0, 0, tiled=True)  25.5 us
    ppermute x4, starting transfers between devices, on_device(): blocks += [block, lax.ppermute(block, 'core', swap)]  22.7 us
    all_to_all x1, blocking collectives, on_device(): lax.all_to_all(part.reshape(Z * YH, share, nb), BAND, 0, 0, tiled=True)  17.4 us
    all_to_all x1, blocking collectives, on_device(): return lax.all_to_all(spread, GA, 0, 0, tiled=True).sum(axis=0)  14.7 us
    all_gather x1, blocking collectives, on_device(): rows = lax.all_gather(rows, 'yl', axis=0, tiled=True)  13.9 us
    ppermute x3, starting transfers between devices, on_device(): lax.ppermute(rows, 'x', [(i, (i - step) % X) for i in range(X)])  9.32 us
    ppermute x1, starting transfers between devices, on_device(): theirs = lax.ppermute(mine, 'yh', swap)  8.27 us
    pallas_call x1, Pallas kernels, on_device(): pl.pallas_call(half_kernel, grid=(rowcount // tile,), out_shape=jax.Shape...  6.88 us
  transfers between devices with their start and end apart: 10, of which 1 were waited for; matrix products, arithmetic and copies ran while one was open for 2% of the time, Pallas kernels for 6%

profile of v2, /device:TPU:1, one launch (start us, length us, event | category | flops | bytes accessed | tf_op | source)
XLA Modules:
  0.0 153.8 jit_solution(12080209040666998914)
XLA Ops:
  6.5 0.0 all-gather.3.cloned.1.call-start
  6.5 8.3 %collective-permute-start = (bf16[48,1152]{1,0:T(8,128)(2,1)}, bf16[48,1152]{1,0:T(8,128)(2,1)S(1)}, u32[]{:S(2)}, u32[]{:S(2)}) collective-permute-start(bf16[48,1152]{1,0:T(8,128)(2,1)} %bitcast.11), channel_id=1, source_target_pairs={{0,32},{32,0},{1,33},{33,1},{2,34},{34,2},{3,35},{35,3},{4,36},{36... | collective-permute-start | bytes 331784 | tf_op jit(solution)/shard_map/ppermute | solution.py:84
  16.2 2.6 %collective-permute-start.1 = (f32[1]{0:T(128)}, f32[1]{0:T(128)}, u32[]{:S(2)}, u32[]{:S(2)}) collective-permute-start(f32[1]{0:T(128)} %div.7), channel_id=1, source_target_pairs={{0,32},{32,0},{1,33},{33,1},{2,34},{34,2},{3,35},{35,3},{4,36},{36... | collective-permute-start | bytes 20 | tf_op jit(solution)/shard_map/ppermute | solution.py:85
  18.8 0.0 collective-permute-done
  18.8 1.6 %pad_maximum_fusion.both_ref = bf16[2,48,1152]{2,1,0:T(8,128)(2,1)} fusion(bf16[1,48,1152]{2,1,0:T(8,128)(2,1)S(1)} %bitcast.12, bf16[1,48,1152]{2,1,0:T(8,128)(2,1)} %param.4), kind=kLoop, calls=%fused_computation | loop fusion | flops 110592 | bytes 442368 | tf_op jit(solution)/shard_map/stack | solution.py:86
  20.4 3.9 %collective-permute-done.1 = f32[1]{0:T(128)} collective-permute-done((f32[1]{0:T(128)}, f32[1]{0:T(128)}, u32[]{:S(2)}, u32[]{:S(2)}) %collective-permute-start.1) | collective-permute-done | bytes 36 | tf_op jit(solution)/shard_map/ppermute | solution.py:85
  24.3 0.0 all-gather.3.cloned.1.call-update
  24.4 0.6 pad_maximum_fusion.1.coef_ref
  25.0 0.0 copy-start.1
  25.0 0.9 copy-done.1
  25.9 0.7 shard_map.48
  26.7 25.5 %all_to_all.15.got_ref = bf16[12,48,96]{2,1,0:T(8,128)(2,1)S(1)} all-to-all(bf16[12,48,96]{2,1,0:T(8,128)(2,1)S(1)} %shard_map.48), channel_id=1, replica_groups=mesh['z'=12,'yh'=2,'x'=4,'yl'=4,'core'=2] {'z'}, dimensions={0} | all-to-all | bytes 221184 | tf_op jit(solution)/shard_map/all_to_all | solution.py:106
  52.2 0.1 shard_map.49
  52.3 13.9 %all_gather.11.refs_0_ = bf16[192,1152]{1,0:T(8,128)(2,1)} all-gather(bf16[48,1152]{1,0:T(8,128)(2,1)S(1)} %shard_map.49), channel_id=1, replica_groups=mesh['z'=12,'yh'=2,'x'=4,'yl'=4,'core'=2] {'yl'}, dimensions={0}, use_global_device_ids=true | all-gather | bytes 552960 | tf_op jit(solution)/shard_map/all_gather | solution.py:114
  66.1 4.4 %collective-permute-start.3 = (bf16[192,1152]{1,0:T(8,128)(2,1)}, bf16[192,1152]{1,0:T(8,128)(2,1)}, u32[]{:S(2)}, u32[]{:S(2)}) collective-permute-start(bf16[192,1152]{1,0:T(8,128)(2,1)} %all_gather.11.refs_0_), channel_id=1, source_target_pairs={{0,24},{8,0},{16,8},{24,16},{1,25},{9,1},{17,9},{25,17},{2,26},{10... | collective-permute-start | bytes 1327112 | tf_op jit(solution)/shard_map/ppermute | solution.py:117
  70.5 2.4 %collective-permute-start.5 = (bf16[192,1152]{1,0:T(8,128)(2,1)}, bf16[192,1152]{1,0:T(8,128)(2,1)}, u32[]{:S(2)}, u32[]{:S(2)}) collective-permute-start(bf16[192,1152]{1,0:T(8,128)(2,1)} %all_gather.11.refs_0_), channel_id=1, source_target_pairs={{0,16},{8,24},{16,0},{24,8},{1,17},{9,25},{17,1},{25,9},{2,18},{10... | collective-permute-start | bytes 1327112 | tf_op jit(solution)/shard_map/ppermute | solution.py:117
  73.0 2.5 %collective-permute-start.7 = (bf16[192,1152]{1,0:T(8,128)(2,1)}, bf16[192,1152]{1,0:T(8,128)(2,1)}, u32[]{:S(2)}, u32[]{:S(2)}) collective-permute-start(bf16[192,1152]{1,0:T(8,128)(2,1)} %all_gather.11.refs_0_), channel_id=1, source_target_pairs={{0,8},{8,16},{16,24},{24,0},{1,9},{9,17},{17,25},{25,1},{2,10},{10... | collective-permute-start | bytes 1327112 | tf_op jit(solution)/shard_map/ppermute | solution.py:117
  75.5 8.4 %collective-permute-start.2 = (bf16[192,1152]{1,0:T(8,128)(2,1)}, bf16[192,1152]{1,0:T(8,128)(2,1)}, u32[]{:S(2)}, u32[]{:S(2)}) collective-permute-start(bf16[192,1152]{1,0:T(8,128)(2,1)} %all_gather.11.refs_0_), channel_id=1, source_target_pairs={{0,1},{1,0},{2,3},{3,2},{4,5},{5,4},{6,7},{7,6},{8,9},{9,8},{10,11... | collective-permute-start | bytes 1327112 | tf_op jit(solution)/shard_map/ppermute | solution.py:118
  83.9 0.0 collective-permute-done.3.refs_2_
  83.9 8.7 %collective-permute-start.4 = (bf16[192,1152]{1,0:T(8,128)(2,1)}, bf16[192,1152]{1,0:T(8,128)(2,1)}, u32[]{:S(2)}, u32[]{:S(2)}) collective-permute-start(bf16[192,1152]{1,0:T(8,128)(2,1)} %collective-permute-done.3.refs_2_), channel_id=1, source_target_pairs={{0,1},{1,0},{2,3},{3,2},{4,5},{5,4},{6,7},{7,6},{8,9},{9,8},{10,11... | collective-permute-start | bytes 1327112 | tf_op jit(solution)/shard_map/ppermute | solution.py:118
  92.6 0.0 collective-permute-done.5.refs_4_
  92.6 1.9 %collective-permute-start.6 = (bf16[192,1152]{1,0:T(8,128)(2,1)}, bf16[192,1152]{1,0:T(8,128)(2,1)}, u32[]{:S(2)}, u32[]{:S(2)}) collective-permute-start(bf16[192,1152]{1,0:T(8,128)(2,1)} %collective-permute-done.5.refs_4_), channel_id=1, source_target_pairs={{0,1},{1,0},{2,3},{3,2},{4,5},{5,4},{6,7},{7,6},{8,9},{9,8},{10,11... | collective-permute-start | bytes 1327112 | tf_op jit(solution)/shard_map/ppermute | solution.py:118
  94.5 0.0 collective-permute-done.7.refs_6_
  94.6 3.6 %collective-permute-start.8 = (bf16[192,1152]{1,0:T(8,128)(2,1)}, bf16[192,1152]{1,0:T(8,128)(2,1)}, u32[]{:S(2)}, u32[]{:S(2)}) collective-permute-start(bf16[192,1152]{1,0:T(8,128)(2,1)} %collective-permute-done.7.refs_6_), channel_id=1, source_target_pairs={{0,1},{1,0},{2,3},{3,2},{4,5},{5,4},{6,7},{7,6},{8,9},{9,8},{10,11... | collective-permute-start | bytes 1327112 | tf_op jit(solution)/shard_map/ppermute | solution.py:118
  98.2 0.1 pad_add_fusion.pos_ref
  98.3 0.0 copy-start
  98.3 2.0 %copy-done = bf16[1,32,48,1152]{3,2,1,0:T(8,128)(2,1)S(1)} copy-done((bf16[1,32,48,1152]{3,2,1,0:T(8,128)(2,1)S(1)}, bf16[1,32,48,1152]{3,2,1,0:T(8,128)(2,1)}, u32[]{:S(2)}) %copy-start) | copy-done | bytes 3538968
  100.3 0.8 shard_map.46.w_ref
  101.1 0.0 all-gather.3.cloned.1.call-done
  101.1 0.0 copy-start.2
  101.1 1.7 %copy-done.2 = bf16[24,48,1152]{2,1,0:T(8,128)(2,1)S(1)} copy-done((bf16[24,48,1152]{2,1,0:T(8,128)(2,1)S(1)}, bf16[24,48,1152]{2,1,0:T(8,128)(2,1)}, u32[]{:S(2)}) %copy-start.2) | copy-done | bytes 2654232
  102.9 6.9 %shard_map.47.half_ref = bf16[1152,1536]{1,0:T(8,128)(2,1)S(1)} custom-call(bf16[1152,1152]{1,0:T(8,128)(2,1)S(1)} %bitcast.10, bf16[1536,1152]{1,0:T(8,128)(2,1)S(1)} %shard_map.46.w_ref), custom_call_target="tpu_custom_call" | custom-call | flops 4076863488 | bytes 10485760 | tf_op jit(solution)/shard_map/pallas_call | solution.py:120
  109.8 0.0 collective-permute-done.2.refs_1_
  109.8 0.0 collective-permute-done.4.refs_3_
  109.8 0.0 collective-permute-done.6.refs_5_
  109.8 0.0 collective-permute-done.8.refs_7_
  109.8 4.4 %shard_map.50 = f32[48,48]{1,0:T(8,128)S(1)} custom-call(bf16[1152,1536]{1,0:T(8,128)(2,1)S(1)} %shard_map.47.half_ref, bf16[192,1152]{1,0:T(8,128)(2,1)} %all_gather.11.refs_0_, bf16[192,1152]{1,0:T(8,128)(2,1)} %collective-permute-done.2.refs_1_, bf16[192,1152]{1,0:T(8,128)(2,1)} %collective-permute-done.3.refs_2_, ...), custom_call_target="tpu_custom_call" | custom-call | flops 1358954496 | bytes 6291456 | tf_op jit(solution)/shard_map/pallas_call | solution.py:134
  114.2 17.4 %all_to_all.16 = f32[24,2,48]{2,1,0:T(2,128)S(1)} all-to-all(f32[24,2,48]{2,1,0:T(2,128)S(1)} %bitcast.9), channel_id=1, replica_groups=mesh['z'=12,'yh'=2,'x'=4,'yl'=4,'core'=2] {'z','yh'}, dimensions={0} | all-to-all | bytes 18432 | tf_op jit(solution)/shard_map/all_to_all | solution.py:146
  131.7 14.7 %all_to_all.17 = f32[32,2,48]{2,1,0:T(2,128)S(1)} all-to-all(f32[32,2,48]{2,1,0:T(2,128)S(1)} %broadcast_in_dim.2), channel_id=1, replica_groups=mesh['z'=12,'yh'=2,'x'=4,'yl'=4,'core'=2] {'x','yl','core'}, dimensions={0} | all-to-all | bytes 24576 | tf_op jit(solution)/shard_map/all_to_all | solution.py:148
  146.4 0.6 reduce_sum.19
  (2 shorter events, 0.0 us)
Async XLA Ops:
  6.5 94.6 %all-gather.3.cloned.1.call-start = ((), (), s32[]{:S(2)}) async-start(), calls=%async_computation.3 | async-start | bytes 2875392 | tf_op jit(solution)/shard_map/all_gather | solution.py:87
  6.5 12.3 %collective-permute-start = (bf16[48,1152]{1,0:T(8,128)(2,1)}, bf16[48,1152]{1,0:T(8,128)(2,1)S(1)}, u32[]{:S(2)}, u32[]{:S(2)}) collective-permute-start(bf16[48,1152]{1,0:T(8,128)(2,1)} %bitcast.11), channel_id=1, source_target_pairs={{0,32},{32,0},{1,33},{33,1},{2,34},{34,2},{3,35},{35,3},{4,36},{36... | collective-permute-start | bytes 331784 | tf_op jit(solution)/shard_map/ppermute | solution.py:84
  16.2 8.1 %collective-permute-start.1 = (f32[1]{0:T(128)}, f32[1]{0:T(128)}, u32[]{:S(2)}, u32[]{:S(2)}) collective-permute-start(f32[1]{0:T(128)} %div.7), channel_id=1, source_target_pairs={{0,32},{32,0},{1,33},{33,1},{2,34},{34,2},{3,35},{35,3},{4,36},{36... | collective-permute-start | bytes 20 | tf_op jit(solution)/shard_map/ppermute | solution.py:85
  25.0 0.9 copy-start.1
  66.1 17.8 %collective-permute-start.3 = (bf16[192,1152]{1,0:T(8,128)(2,1)}, bf16[192,1152]{1,0:T(8,128)(2,1)}, u32[]{:S(2)}, u32[]{:S(2)}) collective-permute-start(bf16[192,1152]{1,0:T(8,128)(2,1)} %all_gather.11.refs_0_), channel_id=1, source_target_pairs={{0,24},{8,0},{16,8},{24,16},{1,25},{9,1},{17,9},{25,17},{2,26},{10... | collective-permute-start | bytes 1327112 | tf_op jit(solution)/shard_map/ppermute | solution.py:117
  70.5 22.1 %collective-permute-start.5 = (bf16[192,1152]{1,0:T(8,128)(2,1)}, bf16[192,1152]{1,0:T(8,128)(2,1)}, u32[]{:S(2)}, u32[]{:S(2)}) collective-permute-start(bf16[192,1152]{1,0:T(8,128)(2,1)} %all_gather.11.refs_0_), channel_id=1, source_target_pairs={{0,16},{8,24},{16,0},{24,8},{1,17},{9,25},{17,1},{25,9},{2,18},{10... | collective-permute-start | bytes 1327112 | tf_op jit(solution)/shard_map/ppermute | solution.py:117
  73.0 21.6 %collective-permute-start.7 = (bf16[192,1152]{1,0:T(8,128)(2,1)}, bf16[192,1152]{1,0:T(8,128)(2,1)}, u32[]{:S(2)}, u32[]{:S(2)}) collective-permute-start(bf16[192,1152]{1,0:T(8,128)(2,1)} %all_gather.11.refs_0_), channel_id=1, source_target_pairs={{0,8},{8,16},{16,24},{24,0},{1,9},{9,17},{17,25},{25,1},{2,10},{10... | collective-permute-start | bytes 1327112 | tf_op jit(solution)/shard_map/ppermute | solution.py:117
  75.5 34.3 %collective-permute-start.2 = (bf16[192,1152]{1,0:T(8,128)(2,1)}, bf16[192,1152]{1,0:T(8,128)(2,1)}, u32[]{:S(2)}, u32[]{:S(2)}) collective-permute-start(bf16[192,1152]{1,0:T(8,128)(2,1)} %all_gather.11.refs_0_), channel_id=1, source_target_pairs={{0,1},{1,0},{2,3},{3,2},{4,5},{5,4},{6,7},{7,6},{8,9},{9,8},{10,11... | collective-permute-start | bytes 1327112 | tf_op jit(solution)/shard_map/ppermute | solution.py:118
  83.9 25.9 %collective-permute-start.4 = (bf16[192,1152]{1,0:T(8,128)(2,1)}, bf16[192,1152]{1,0:T(8,128)(2,1)}, u32[]{:S(2)}, u32[]{:S(2)}) collective-permute-start(bf16[192,1152]{1,0:T(8,128)(2,1)} %collective-permute-done.3.refs_2_), channel_id=1, source_target_pairs={{0,1},{1,0},{2,3},{3,2},{4,5},{5,4},{6,7},{7,6},{8,9},{9,8},{10,11... | collective-permute-start | bytes 1327112 | tf_op jit(solution)/shard_map/ppermute | solution.py:118
  92.6 17.2 %collective-permute-start.6 = (bf16[192,1152]{1,0:T(8,128)(2,1)}, bf16[192,1152]{1,0:T(8,128)(2,1)}, u32[]{:S(2)}, u32[]{:S(2)}) collective-permute-start(bf16[192,1152]{1,0:T(8,128)(2,1)} %collective-permute-done.5.refs_4_), channel_id=1, source_target_pairs={{0,1},{1,0},{2,3},{3,2},{4,5},{5,4},{6,7},{7,6},{8,9},{9,8},{10,11... | collective-permute-start | bytes 1327112 | tf_op jit(solution)/shard_map/ppermute | solution.py:118
  94.6 15.2 %collective-permute-start.8 = (bf16[192,1152]{1,0:T(8,128)(2,1)}, bf16[192,1152]{1,0:T(8,128)(2,1)}, u32[]{:S(2)}, u32[]{:S(2)}) collective-permute-start(bf16[192,1152]{1,0:T(8,128)(2,1)} %collective-permute-done.7.refs_6_), channel_id=1, source_target_pairs={{0,1},{1,0},{2,3},{3,2},{4,5},{5,4},{6,7},{7,6},{8,9},{9,8},{10,11... | collective-permute-start | bytes 1327112 | tf_op jit(solution)/shard_map/ppermute | solution.py:118
  98.3 2.0 %copy-start = (bf16[1,32,48,1152]{3,2,1,0:T(8,128)(2,1)S(1)}, bf16[1,32,48,1152]{3,2,1,0:T(8,128)(2,1)}, u32[]{:S(2)}) copy-start(bf16[1,32,48,1152]{3,2,1,0:T(8,128)(2,1)} %param.7) | copy-start | bytes 10616836
  101.1 1.8 %copy-start.2 = (bf16[24,48,1152]{2,1,0:T(8,128)(2,1)S(1)}, bf16[24,48,1152]{2,1,0:T(8,128)(2,1)}, u32[]{:S(2)}) copy-start(bf16[24,48,1152]{2,1,0:T(8,128)(2,1)} %all-gather.3.cloned.1.call-done) | copy-start | bytes 7962628
Sparse Core Ops, SparseCore 0:
  24.5 62.2 all-gather.2

commit v3 on v1

v3 whole, which is shorter than its diff:
```python
import jax
import jax.numpy as jnp
from jax import lax
from jax.experimental import pallas as pl
from jax.experimental.pallas import tpu as pltpu
from jax.sharding import Mesh
from jax.sharding import PartitionSpec as P

NFREQ = 16
Z, YH, X, YL, CORE = 12, 2, 4, 4, 2
BAND = ("z", "yh")
GA = ("x", "yl", "core")
GROUP = 8
VMEM = pl.BlockSpec(memory_space=pltpu.VMEM)
SMEM = pl.BlockSpec(memory_space=pltpu.SMEM)
PARAMS = pltpu.CompilerParams(vmem_limit_bytes=16 << 20)


def turn_kernel(x_ref, core_ref, _, w_ref, out_ref):
    rows = [
        w_ref[(lax.rem(x_ref[0] + step, X) * YL + yl) * CORE + core]
        for step in range(X)
        for core in (core_ref[0], 1 - core_ref[0])
        for yl in range(YL)
    ]
    out_ref[...] = jnp.concatenate(rows, axis=0).T


def pieces_kernel(coef_ref, mine_ref, out_ref):
    count, depth, _ = out_ref.shape
    turned = (mine_ref[...].astype(jnp.float32) * coef_ref[0]).T
    for z in range(count):
        start = z * YH * depth
        halves = [turned[start + i * depth : start + (i + 1) * depth] for i in range(YH)]
        out_ref[z] = jnp.concatenate(halves, axis=1).astype(out_ref.dtype)


def split_kernel(yh_ref, got_ref, keep_ref, give_ref):
    nb = got_ref.shape[2] // YH
    pieces = [got_ref[z].astype(jnp.float32) for z in range(Z)]
    halves = [
        jnp.concatenate([p[:, i * nb : (i + 1) * nb] for p in pieces], axis=1) for i in range(YH)
    ]
    first = yh_ref[0] == 0
    keep_ref[...] = jnp.where(first, halves[0], halves[1]).astype(keep_ref.dtype)
    give_ref[...] = jnp.where(first, halves[1], halves[0]).astype(give_ref.dtype)


def join_kernel(keep_ref, came_ref, out_ref):
    parts = [keep_ref[...].astype(jnp.float32), came_ref[...].astype(jnp.float32)]
    out_ref[...] = jnp.concatenate(parts, axis=1).astype(out_ref.dtype)


def proj_kernel(wt_ref, *refs):
    row_refs, out_ref = refs[:-1], refs[-1]
    tile = GROUP * (out_ref.shape[1] // (Z * YH))
    for g in range(out_ref.shape[1] // tile):
        span = slice(g * tile, (g + 1) * tile)
        rows = jnp.concatenate([r[:, span] for r in row_refs], axis=0)
        out_ref[:, span] = jnp.dot(
            wt_ref[...], rows, preferred_element_type=jnp.float32
        ).astype(out_ref.dtype)


def sigma_kernel(cols_ref, proj_ref, out_ref, cols_buf, proj_buf, sems):
    nb = out_ref.shape[0]
    groups, _, _, width = cols_buf.shape
    tile = GROUP * nb
    copies = []
    for g in range(groups):
        parts = [(proj_ref.at[:, pl.ds(g * tile, tile)], proj_buf.at[g])]
        for side in range(YH):
            low, high = max(g * GROUP, side * Z), min((g + 1) * GROUP, (side + 1) * Z)
            if low < high:
                parts.append(
                    (
                        cols_ref.at[pl.ds(low - side * Z, high - low), side],
                        cols_buf.at[g, pl.ds(low - g * GROUP, high - low)],
                    )
                )
        copies.append([pltpu.make_async_copy(a, b, sems.at[g, i]) for i, (a, b) in enumerate(parts)])
    for copy in sum(copies, []):
        copy.start()
    sigma = jnp.zeros((nb, nb), jnp.float32)
    for g in range(groups):
        for copy in copies[g]:
            copy.wait()
        block = jnp.dot(
            cols_buf[g].reshape(tile, width), proj_buf[g], preferred_element_type=jnp.float32
        )
        for i in range(GROUP):
            sigma += block[i * nb : (i + 1) * nb, i * nb : (i + 1) * nb]
    out_ref[...] = sigma.T


def on_device(pair_dens, energies, freq_index, screened):
    mine = pair_dens[0]
    nb, width = mine.shape
    sub = width // (Z * YH)
    rowcount = X * YL * CORE * sub
    mcols = Z * YH * nb
    tile = GROUP * nb
    place = {axis: lax.axis_index(axis).astype(jnp.int32).reshape(1) for axis in ("yh", "x", "core")}
    swap = [(0, 1), (1, 0)]

    omega = 0.1 * jnp.exp(jnp.log(20.0) * freq_index[0].astype(jnp.float32) / (NFREQ - 1))
    coef = energies / (energies * energies + omega * omega)
    pieces = pl.pallas_call(
        pieces_kernel,
        out_shape=jax.ShapeDtypeStruct((Z, sub, YH * nb), jnp.bfloat16),
        in_specs=[SMEM, VMEM],
        out_specs=VMEM,
        compiler_params=PARAMS,
    )(coef, mine)
    got = lax.all_to_all(pieces, "z", 0, 0, tiled=True)

    theirs = lax.ppermute(mine, "yh", swap)
    both, got = lax.optimization_barrier((jnp.stack([mine, theirs]), got))
    cols = lax.all_gather(both, "z")

    keep, give = pl.pallas_call(
        split_kernel,
        out_shape=[jax.ShapeDtypeStruct((sub, Z * nb), jnp.bfloat16)] * 2,
        in_specs=[SMEM, VMEM],
        out_specs=[VMEM] * 2,
        compiler_params=PARAMS,
    )(place["yh"], got)
    turned = pl.pallas_call(
        turn_kernel,
        out_shape=jax.ShapeDtypeStruct((width, rowcount), jnp.bfloat16),
        in_specs=[SMEM, SMEM, pl.BlockSpec(memory_space=pl.ANY), VMEM],
        out_specs=VMEM,
        compiler_params=PARAMS,
        cost_estimate=pl.CostEstimate(flops=0, bytes_accessed=4 * rowcount * width, transcendentals=0),
    )(place["x"], place["core"], keep, screened[0])
    came, turned = lax.optimization_barrier((lax.ppermute(give, "yh", swap), turned))
    rows = pl.pallas_call(
        join_kernel,
        out_shape=jax.ShapeDtypeStruct((sub, mcols), jnp.bfloat16),
        in_specs=[VMEM] * 2,
        out_specs=VMEM,
        compiler_params=PARAMS,
    )(keep, came)
    rows = lax.all_gather(rows, "yl", axis=0, tiled=True)
    blocks = []
    for step in range(X):
        block = rows if step == 0 else lax.ppermute(rows, "x", [(i, (i - step) % X) for i in range(X)])
        blocks += [block, lax.ppermute(block, "core", swap)]

    proj = pl.pallas_call(
        proj_kernel,
        out_shape=jax.ShapeDtypeStruct((width, mcols), jnp.bfloat16),
        in_specs=[VMEM] * (1 + len(blocks)),
        out_specs=VMEM,
        compiler_params=PARAMS,
        cost_estimate=pl.CostEstimate(
            flops=2 * width * mcols * rowcount, bytes_accessed=10 << 20, transcendentals=0
        ),
    )(turned, *blocks)
    part = pl.pallas_call(
        sigma_kernel,
        out_shape=jax.ShapeDtypeStruct((nb, nb), jnp.float32),
        in_specs=[pl.BlockSpec(memory_space=pl.ANY)] * 2,
        out_specs=VMEM,
        scratch_shapes=[
            pltpu.VMEM((mcols // tile, GROUP, nb, width), jnp.bfloat16),
            pltpu.VMEM((mcols // tile, width, tile), jnp.bfloat16),
            pltpu.SemaphoreType.DMA((mcols // tile, 1 + YH)),
        ],
        compiler_params=pltpu.CompilerParams(vmem_limit_bytes=60 << 20),
        cost_estimate=pl.CostEstimate(
            flops=2 * width * mcols * tile, bytes_accessed=6 << 20, transcendentals=0
        ),
    )(cols, proj)

    share = nb // (Z * YH)
    part = lax.all_to_all(part.reshape(Z * YH, share, nb), BAND, 0, 0, tiled=True).sum(axis=0)
    spread = jnp.broadcast_to(part[None], (X * YL * CORE, share, nb))
    return lax.all_to_all(spread, GA, 0, 0, tiled=True).sum(axis=0)


def solution(mesh):
    fine = Mesh(mesh.devices.reshape(Z, YH, X, YL, CORE), BAND + GA)
    return jax.shard_map(
        on_device,
        mesh=fine,
        in_specs=(P(BAND, None, GA), P(BAND), P(), P(BAND, None, None, GA)),
        out_specs=P(BAND, None),
        check_vma=False,
    )
```

time: 215 us -> 152 us (0.71)
  waiting for transfers between devices: 75.2 us -> 15 us
  starting transfers between devices: 5.7 us -> 56.8 us
  blocking collectives: 93.1 us -> 45.9 us
  local copies, waits for them, and re-layouts: 11.1 us -> 4.42 us
    all_gather x2 -> x1, waiting for transfers between devices: 65.4 us -> 0.01 us  [on_device(): cols = lax.all_gather(both, 'z')]
    ppermute x2 -> x9, starting transfers between devices: 5.66 us -> 41.9 us  [the longest x4 22.3 us: on_device(): blocks += [block, lax.ppermute(block, 'core', swap)]]
    all_to_all x1 -> x0, blocking collectives: 35 us -> none  [on_device(): got = lax.all_to_all(pieces, BAND, 0, 0, tiled=True)]
    all_to_all x0 -> x1, starting transfers between devices: none -> 14.9 us  [on_device(): got = lax.all_to_all(pieces, 'z', 0, 0, tiled=True)]
    all_to_all x0 -> x1, waiting for transfers between devices: none -> 9.11 us  [on_device(): got = lax.all_to_all(pieces, 'z', 0, 0, tiled=True)]
    all_to_all x1, blocking collectives: 24.2 us -> 18.6 us  [on_device(): lax.all_to_all(part.reshape(Z * YH, share, nb), BAND, 0, 0, tiled=True)]
    all_to_all x1, blocking collectives: 19.9 us -> 14.9 us  [on_device(): return lax.all_to_all(spread, GA, 0, 0, tiled=True).sum(axis=0)]
    ppermute x2 -> x9, waiting for transfers between devices: 9.82 us -> 5.84 us  [the longest x1 4.45 us: on_device(): lax.ppermute(give, 'yh', swap)]
  transfers between devices with their start and end apart: 4 -> 11, of which waited for: 4 -> 3; matrix products, arithmetic and copies ran while one was open for 1% -> 1% of each run, Pallas kernels for 4% -> 5%
where the time goes in v3:
time: 152 us
  starting transfers between devices  56.8 us (37%)
  blocking collectives  45.9 us (30%)
  waiting for transfers between devices  15 us (10%)
  between operations  15 us (10%)
  Pallas kernels  12.1 us (8%)
  local copies, waits for them, and re-layouts  4.42 us (3%)
  other arithmetic  2.27 us (1%)
    ppermute x4, starting transfers between devices, on_device(): blocks += [block, lax.ppermute(block, 'core', swap)]  22.3 us
    all_to_all x1, blocking collectives, on_device(): lax.all_to_all(part.reshape(Z * YH, share, nb), BAND, 0, 0, tiled=True)  18.6 us
    all_to_all x1, blocking collectives, on_device(): return lax.all_to_all(spread, GA, 0, 0, tiled=True).sum(axis=0)  14.9 us
    all_to_all x1, starting transfers between devices, on_device(): got = lax.all_to_all(pieces, 'z', 0, 0, tiled=True)  14.9 us
    all_gather x1, blocking collectives, on_device(): rows = lax.all_gather(rows, 'yl', axis=0, tiled=True)  12.4 us
    ppermute x3, starting transfers between devices, on_device(): lax.ppermute(rows, 'x', [(i, (i - step) % X) for i in range(X)])  9.32 us
    all_to_all x1, waiting for transfers between devices, on_device(): got = lax.all_to_all(pieces, 'z', 0, 0, tiled=True)  9.11 us
    ppermute x1, starting transfers between devices, on_device(): theirs = lax.ppermute(mine, 'yh', swap)  8.27 us
  transfers between devices with their start and end apart: 11, of which 3 were waited for; matrix products, arithmetic and copies ran while one was open for 1% of the time, Pallas kernels for 5%

profile of v3, /device:TPU:1, one launch (start us, length us, event | category | flops | bytes accessed | tf_op | source)
XLA Modules:
  0.0 151.5 jit_solution(2237916797053579647)
XLA Ops:
  6.5 8.3 %collective-permute-start = (bf16[48,1152]{1,0:T(8,128)(2,1)}, bf16[48,1152]{1,0:T(8,128)(2,1)S(1)}, u32[]{:S(2)}, u32[]{:S(2)}) collective-permute-start(bf16[48,1152]{1,0:T(8,128)(2,1)} %bitcast.9), channel_id=1, source_target_pairs={{0,32},{32,0},{1,33},{33,1},{2,34},{34,2},{3,35},{35,3},{4,36},{36... | collective-permute-start | bytes 331784 | tf_op jit(solution)/shard_map/ppermute | solution.py:117
  16.2 0.0 copy-start.2
  16.2 0.9 copy-done.2
  17.1 0.9 shard_map.46
  18.0 14.9 %all-to-all-start = ((bf16[12,48,96]{2,1,0:T(8,128)(2,1)}), bf16[12,48,96]{2,1,0:T(8,128)(2,1)S(1)}, u32[]{:S(2)}, u32[]{:S(2)}) async-start(bf16[12,48,96]{2,1,0:T(8,128)(2,1)} %shard_map.46), calls=%async_computation | async-start | bytes 294912 | tf_op jit(solution)/shard_map/all_to_all | solution.py:115
  32.9 0.0 all-gather.3.cloned.1.call-start
  32.9 0.0 collective-permute-done
  32.9 1.6 %pad_maximum_fusion = bf16[2,48,1152]{2,1,0:T(8,128)(2,1)} fusion(bf16[1,48,1152]{2,1,0:T(8,128)(2,1)S(1)} %bitcast.12, bf16[1,48,1152]{2,1,0:T(8,128)(2,1)} %param.4), kind=kLoop, calls=%fused_computation | loop fusion | flops 110592 | bytes 442368 | tf_op jit(solution)/shard_map/stack | solution.py:118
  34.6 9.1 %all-to-all-done.got_ref = bf16[12,48,96]{2,1,0:T(8,128)(2,1)S(1)} async-done(((bf16[12,48,96]{2,1,0:T(8,128)(2,1)}), bf16[12,48,96]{2,1,0:T(8,128)(2,1)S(1)}, u32[]{:S(2)}, u32[]{:S(2)}) %all-to-all-start) | async-done | bytes 110624 | tf_op jit(solution)/shard_map/all_to_all | solution.py:115
  43.7 0.0 all-gather.3.cloned.1.call-update
  43.7 0.1 shard_map.47
  43.9 2.0 %collective-permute-start.1 = (bf16[48,576]{1,0:T(8,128)(2,1)S(1)}, bf16[48,576]{1,0:T(8,128)(2,1)S(1)}, u32[]{:S(2)}, u32[]{:S(2)}) collective-permute-start(bf16[48,576]{1,0:T(8,128)(2,1)S(1)} %get-tuple-element.13), channel_id=1, source_target_pairs={{0,32},{32,0},{1,33},{33,1},{2,34},{34,2},{3,35},{35,3},{4,36},{36... | collective-permute-start | bytes 165896 | tf_op jit(solution)/shard_map/ppermute | solution.py:136
  45.8 0.0 copy-start
  45.9 2.0 %copy-done = bf16[1,32,48,1152]{3,2,1,0:T(8,128)(2,1)S(1)} copy-done((bf16[1,32,48,1152]{3,2,1,0:T(8,128)(2,1)S(1)}, bf16[1,32,48,1152]{3,2,1,0:T(8,128)(2,1)}, u32[]{:S(2)}) %copy-start) | copy-done | bytes 3538968
  47.8 1.0 shard_map.48.wt_ref
  48.8 4.5 %collective-permute-done.1.came_ref = bf16[48,576]{1,0:T(8,128)(2,1)S(1)} collective-permute-done((bf16[48,576]{1,0:T(8,128)(2,1)S(1)}, bf16[48,576]{1,0:T(8,128)(2,1)S(1)}, u32[]{:S(2)}, u32[]{:S(2)}) %collective-permute-start.1) | collective-permute-done | bytes 55328 | tf_op jit(solution)/shard_map/ppermute | solution.py:136
  53.3 0.1 shard_map.49
  53.4 12.4 %all_gather.11.refs_0_ = bf16[192,1152]{1,0:T(8,128)(2,1)S(1)} all-gather(bf16[48,1152]{1,0:T(8,128)(2,1)S(1)} %shard_map.49), channel_id=1, replica_groups=mesh['z'=12,'yh'=2,'x'=4,'yl'=4,'core'=2] {'yl'}, dimensions={0}, use_global_device_ids=true | all-gather | bytes 552960 | tf_op jit(solution)/shard_map/all_gather | solution.py:144
  65.8 4.4 %collective-permute-start.3 = (bf16[192,1152]{1,0:T(8,128)(2,1)S(1)}, bf16[192,1152]{1,0:T(8,128)(2,1)S(1)}, u32[]{:S(2)}, u32[]{:S(2)}) collective-permute-start(bf16[192,1152]{1,0:T(8,128)(2,1)S(1)} %all_gather.11.refs_0_), channel_id=1, source_target_pairs={{0,24},{8,0},{16,8},{24,16},{1,25},{9,1},{17,9},{25,17},{2,26},{10... | collective-permute-start | bytes 1327112 | tf_op jit(solution)/shard_map/ppermute | solution.py:147
  70.1 2.4 %collective-permute-start.5 = (bf16[192,1152]{1,0:T(8,128)(2,1)S(1)}, bf16[192,1152]{1,0:T(8,128)(2,1)S(1)}, u32[]{:S(2)}, u32[]{:S(2)}) collective-permute-start(bf16[192,1152]{1,0:T(8,128)(2,1)S(1)} %all_gather.11.refs_0_), channel_id=1, source_target_pairs={{0,16},{8,24},{16,0},{24,8},{1,17},{9,25},{17,1},{25,9},{2,18},{10... | collective-permute-start | bytes 1327112 | tf_op jit(solution)/shard_map/ppermute | solution.py:147
  72.6 2.5 %collective-permute-start.7 = (bf16[192,1152]{1,0:T(8,128)(2,1)S(1)}, bf16[192,1152]{1,0:T(8,128)(2,1)S(1)}, u32[]{:S(2)}, u32[]{:S(2)}) collective-permute-start(bf16[192,1152]{1,0:T(8,128)(2,1)S(1)} %all_gather.11.refs_0_), channel_id=1, source_target_pairs={{0,8},{8,16},{16,24},{24,0},{1,9},{9,17},{17,25},{25,1},{2,10},{10... | collective-permute-start | bytes 1327112 | tf_op jit(solution)/shard_map/ppermute | solution.py:147
  75.1 9.1 %collective-permute-start.2 = (bf16[192,1152]{1,0:T(8,128)(2,1)S(1)}, bf16[192,1152]{1,0:T(8,128)(2,1)S(1)}, u32[]{:S(2)}, u32[]{:S(2)}) collective-permute-start(bf16[192,1152]{1,0:T(8,128)(2,1)S(1)} %all_gather.11.refs_0_), channel_id=1, source_target_pairs={{0,1},{1,0},{2,3},{3,2},{4,5},{5,4},{6,7},{7,6},{8,9},{9,8},{10,11... | collective-permute-start | bytes 1327112 | tf_op jit(solution)/shard_map/ppermute | solution.py:148
  84.2 0.0 collective-permute-done.3.refs_2_
  84.2 7.7 %collective-permute-start.4 = (bf16[192,1152]{1,0:T(8,128)(2,1)S(1)}, bf16[192,1152]{1,0:T(8,128)(2,1)S(1)}, u32[]{:S(2)}, u32[]{:S(2)}) collective-permute-start(bf16[192,1152]{1,0:T(8,128)(2,1)S(1)} %collective-permute-done.3.refs_2_), channel_id=1, source_target_pairs={{0,1},{1,0},{2,3},{3,2},{4,5},{5,4},{6,7},{7,6},{8,9},{9,8},{10,11... | collective-permute-start | bytes 1327112 | tf_op jit(solution)/shard_map/ppermute | solution.py:148
  91.9 0.0 collective-permute-done.5.refs_4_
  91.9 1.9 %collective-permute-start.6 = (bf16[192,1152]{1,0:T(8,128)(2,1)S(1)}, bf16[192,1152]{1,0:T(8,128)(2,1)S(1)}, u32[]{:S(2)}, u32[]{:S(2)}) collective-permute-start(bf16[192,1152]{1,0:T(8,128)(2,1)S(1)} %collective-permute-done.5.refs_4_), channel_id=1, source_target_pairs={{0,1},{1,0},{2,3},{3,2},{4,5},{5,4},{6,7},{7,6},{8,9},{9,8},{10,11... | collective-permute-start | bytes 1327112 | tf_op jit(solution)/shard_map/ppermute | solution.py:148
  93.8 0.0 collective-permute-done.7.refs_6_
  93.9 3.6 %collective-permute-start.8 = (bf16[192,1152]{1,0:T(8,128)(2,1)S(1)}, bf16[192,1152]{1,0:T(8,128)(2,1)S(1)}, u32[]{:S(2)}, u32[]{:S(2)}) collective-permute-start(bf16[192,1152]{1,0:T(8,128)(2,1)S(1)} %collective-permute-done.7.refs_6_), channel_id=1, source_target_pairs={{0,1},{1,0},{2,3},{3,2},{4,5},{5,4},{6,7},{7,6},{8,9},{9,8},{10,11... | collective-permute-start | bytes 1327112 | tf_op jit(solution)/shard_map/ppermute | solution.py:148
  97.5 0.0 collective-permute-done.2.refs_1_
  97.5 0.0 collective-permute-done.4.refs_3_
  97.5 0.0 collective-permute-done.6.refs_5_
  97.5 1.4 collective-permute-done.8.refs_7_
  98.9 5.7 %shard_map.50.proj_ref = bf16[1152,1152]{1,0:T(8,128)(2,1)S(1)} custom-call(bf16[1152,1536]{1,0:T(8,128)(2,1)S(1)} %shard_map.48.wt_ref, bf16[192,1152]{1,0:T(8,128)(2,1)S(1)} %all_gather.11.refs_0_, bf16[192,1152]{1,0:T(8,128)(2,1)S(1)} %collective-permute-done.2.refs_1_, bf16[192,1152]{1,0:T(8,128)(2,1)S(1)} %collective-permute-done.3.refs_2_, ...), custom_call_target="tpu_custom_call" | custom-call | flops 4076863488 | bytes 10485760 | tf_op jit(solution)/shard_map/pallas_call | solution.py:150
  104.6 0.0 copy-start.1
  104.6 1.5 %copy-done.1 = bf16[1152,1152]{1,0:T(8,128)(2,1)} copy-done((bf16[1152,1152]{1,0:T(8,128)(2,1)}, bf16[1152,1152]{1,0:T(8,128)(2,1)S(1)}, u32[]{:S(2)}) %copy-start.1) | copy-done | bytes 2654232
  106.1 0.0 all-gather.3.cloned.1.call-done
  106.1 4.4 %shard_map.51 = f32[48,48]{1,0:T(8,128)} custom-call(bf16[12,2,48,1152]{3,2,1,0:T(8,128)(2,1)} %bitcast.11, bf16[1152,1152]{1,0:T(8,128)(2,1)} %copy-done.1), custom_call_target="tpu_custom_call" | custom-call | flops 1019215872 | bytes 6291456 | tf_op jit(solution)/shard_map/pallas_call | solution.py:160
  110.5 18.6 %all_to_all.15 = f32[24,2,48]{2,1,0:T(2,128)S(1)} all-to-all(f32[24,2,48]{2,1,0:T(2,128)} %bitcast.13), channel_id=1, replica_groups=mesh['z'=12,'yh'=2,'x'=4,'yl'=4,'core'=2] {'z','yh'}, dimensions={0} | all-to-all | bytes 18432 | tf_op jit(solution)/shard_map/all_to_all | solution.py:177
  129.1 14.9 %all_to_all.16 = f32[32,2,48]{2,1,0:T(2,128)S(1)} all-to-all(f32[32,2,48]{2,1,0:T(2,128)S(1)} %broadcast_in_dim.2), channel_id=1, replica_groups=mesh['z'=12,'yh'=2,'x'=4,'yl'=4,'core'=2] {'x','yl','core'}, dimensions={0} | all-to-all | bytes 24576 | tf_op jit(solution)/shard_map/all_to_all | solution.py:179
  144.1 0.6 reduce_sum.19
  (2 shorter events, 0.0 us)
Async XLA Ops:
  6.5 26.4 %collective-permute-start = (bf16[48,1152]{1,0:T(8,128)(2,1)}, bf16[48,1152]{1,0:T(8,128)(2,1)S(1)}, u32[]{:S(2)}, u32[]{:S(2)}) collective-permute-start(bf16[48,1152]{1,0:T(8,128)(2,1)} %bitcast.9), channel_id=1, source_target_pairs={{0,32},{32,0},{1,33},{33,1},{2,34},{34,2},{3,35},{35,3},{4,36},{36... | collective-permute-start | bytes 331784 | tf_op jit(solution)/shard_map/ppermute | solution.py:117
  16.2 0.9 copy-start.2
  18.0 25.7 %all-to-all-start = ((bf16[12,48,96]{2,1,0:T(8,128)(2,1)}), bf16[12,48,96]{2,1,0:T(8,128)(2,1)S(1)}, u32[]{:S(2)}, u32[]{:S(2)}) async-start(bf16[12,48,96]{2,1,0:T(8,128)(2,1)} %shard_map.46), calls=%async_computation | async-start | bytes 294912 | tf_op jit(solution)/shard_map/all_to_all | solution.py:115
  32.9 73.2 %all-gather.3.cloned.1.call-start = ((), (), s32[]{:S(2)}) async-start(), calls=%async_computation.3 | async-start | bytes 2875392 | tf_op jit(solution)/shard_map/all_gather | solution.py:119
  43.9 9.4 %collective-permute-start.1 = (bf16[48,576]{1,0:T(8,128)(2,1)S(1)}, bf16[48,576]{1,0:T(8,128)(2,1)S(1)}, u32[]{:S(2)}, u32[]{:S(2)}) collective-permute-start(bf16[48,576]{1,0:T(8,128)(2,1)S(1)} %get-tuple-element.13), channel_id=1, source_target_pairs={{0,32},{32,0},{1,33},{33,1},{2,34},{34,2},{3,35},{35,3},{4,36},{36... | collective-permute-start | bytes 165896 | tf_op jit(solution)/shard_map/ppermute | solution.py:136
  45.8 2.0 %copy-start = (bf16[1,32,48,1152]{3,2,1,0:T(8,128)(2,1)S(1)}, bf16[1,32,48,1152]{3,2,1,0:T(8,128)(2,1)}, u32[]{:S(2)}) copy-start(bf16[1,32,48,1152]{3,2,1,0:T(8,128)(2,1)} %param.7) | copy-start | bytes 10616836
  65.8 18.4 %collective-permute-start.3 = (bf16[192,1152]{1,0:T(8,128)(2,1)S(1)}, bf16[192,1152]{1,0:T(8,128)(2,1)S(1)}, u32[]{:S(2)}, u32[]{:S(2)}) collective-permute-start(bf16[192,1152]{1,0:T(8,128)(2,1)S(1)} %all_gather.11.refs_0_), channel_id=1, source_target_pairs={{0,24},{8,0},{16,8},{24,16},{1,25},{9,1},{17,9},{25,17},{2,26},{10... | collective-permute-start | bytes 1327112 | tf_op jit(solution)/shard_map/ppermute | solution.py:147
  70.1 21.8 %collective-permute-start.5 = (bf16[192,1152]{1,0:T(8,128)(2,1)S(1)}, bf16[192,1152]{1,0:T(8,128)(2,1)S(1)}, u32[]{:S(2)}, u32[]{:S(2)}) collective-permute-start(bf16[192,1152]{1,0:T(8,128)(2,1)S(1)} %all_gather.11.refs_0_), channel_id=1, source_target_pairs={{0,16},{8,24},{16,0},{24,8},{1,17},{9,25},{17,1},{25,9},{2,18},{10... | collective-permute-start | bytes 1327112 | tf_op jit(solution)/shard_map/ppermute | solution.py:147
  72.6 21.3 %collective-permute-start.7 = (bf16[192,1152]{1,0:T(8,128)(2,1)S(1)}, bf16[192,1152]{1,0:T(8,128)(2,1)S(1)}, u32[]{:S(2)}, u32[]{:S(2)}) collective-permute-start(bf16[192,1152]{1,0:T(8,128)(2,1)S(1)} %all_gather.11.refs_0_), channel_id=1, source_target_pairs={{0,8},{8,16},{16,24},{24,0},{1,9},{9,17},{17,25},{25,1},{2,10},{10... | collective-permute-start | bytes 1327112 | tf_op jit(solution)/shard_map/ppermute | solution.py:147
  75.1 22.4 %collective-permute-start.2 = (bf16[192,1152]{1,0:T(8,128)(2,1)S(1)}, bf16[192,1152]{1,0:T(8,128)(2,1)S(1)}, u32[]{:S(2)}, u32[]{:S(2)}) collective-permute-start(bf16[192,1152]{1,0:T(8,128)(2,1)S(1)} %all_gather.11.refs_0_), channel_id=1, source_target_pairs={{0,1},{1,0},{2,3},{3,2},{4,5},{5,4},{6,7},{7,6},{8,9},{9,8},{10,11... | collective-permute-start | bytes 1327112 | tf_op jit(solution)/shard_map/ppermute | solution.py:148
  84.2 13.3 %collective-permute-start.4 = (bf16[192,1152]{1,0:T(8,128)(2,1)S(1)}, bf16[192,1152]{1,0:T(8,128)(2,1)S(1)}, u32[]{:S(2)}, u32[]{:S(2)}) collective-permute-start(bf16[192,1152]{1,0:T(8,128)(2,1)S(1)} %collective-permute-done.3.refs_2_), channel_id=1, source_target_pairs={{0,1},{1,0},{2,3},{3,2},{4,5},{5,4},{6,7},{7,6},{8,9},{9,8},{10,11... | collective-permute-start | bytes 1327112 | tf_op jit(solution)/shard_map/ppermute | solution.py:148
  91.9 5.6 %collective-permute-start.6 = (bf16[192,1152]{1,0:T(8,128)(2,1)S(1)}, bf16[192,1152]{1,0:T(8,128)(2,1)S(1)}, u32[]{:S(2)}, u32[]{:S(2)}) collective-permute-start(bf16[192,1152]{1,0:T(8,128)(2,1)S(1)} %collective-permute-done.5.refs_4_), channel_id=1, source_target_pairs={{0,1},{1,0},{2,3},{3,2},{4,5},{5,4},{6,7},{7,6},{8,9},{9,8},{10,11... | collective-permute-start | bytes 1327112 | tf_op jit(solution)/shard_map/ppermute | solution.py:148
  93.9 5.0 %collective-permute-start.8 = (bf16[192,1152]{1,0:T(8,128)(2,1)S(1)}, bf16[192,1152]{1,0:T(8,128)(2,1)S(1)}, u32[]{:S(2)}, u32[]{:S(2)}) collective-permute-start(bf16[192,1152]{1,0:T(8,128)(2,1)S(1)} %collective-permute-done.7.refs_6_), channel_id=1, source_target_pairs={{0,1},{1,0},{2,3},{3,2},{4,5},{5,4},{6,7},{7,6},{8,9},{9,8},{10,11... | collective-permute-start | bytes 1327112 | tf_op jit(solution)/shard_map/ppermute | solution.py:148
  104.6 1.5 %copy-start.1 = (bf16[1152,1152]{1,0:T(8,128)(2,1)}, bf16[1152,1152]{1,0:T(8,128)(2,1)S(1)}, u32[]{:S(2)}) copy-start(bf16[1152,1152]{1,0:T(8,128)(2,1)S(1)} %shard_map.50.proj_ref) | copy-start | bytes 7962628
Sparse Core Ops, SparseCore 0:
  43.8 48.5 all-gather.2

commit v4 on v3

v4 whole, which is shorter than its diff:
```python
import math

import jax
import jax.numpy as jnp
from jax import lax
from jax.experimental import pallas as pl
from jax.experimental.pallas import tpu as pltpu
from jax.sharding import Mesh
from jax.sharding import PartitionSpec as P

NFREQ = 16
Z, YH, X, YL, CORE = 12, 2, 4, 4, 2
BAND = ("z", "yh")
GA = ("x", "yl", "core")
GROUP = 8
VMEM = pl.BlockSpec(memory_space=pltpu.VMEM)
SMEM = pl.BlockSpec(memory_space=pltpu.SMEM)
PARAMS = pltpu.CompilerParams(vmem_limit_bytes=16 << 20)


def turn_kernel(x_ref, core_ref, _, w_ref, out_ref):
    rows = [
        w_ref[(lax.rem(x_ref[0] + step, X) * YL + yl) * CORE + core]
        for step in range(X)
        for core in (core_ref[0], 1 - core_ref[0])
        for yl in range(YL)
    ]
    out_ref[...] = jnp.concatenate(rows, axis=0).T


def label_kernel(energy_ref, mine_ref, out_ref):
    nb, width = mine_ref.shape
    out_ref[:nb, :] = mine_ref[...]
    shape = (out_ref.shape[0] - nb, width)
    energy = jnp.full(shape, energy_ref[0], jnp.float32)
    high = energy.astype(jnp.bfloat16).astype(jnp.float32)
    middle = (energy - high).astype(jnp.bfloat16).astype(jnp.float32)
    low = energy - high - middle
    lane = lax.broadcasted_iota(jnp.int32, shape, 1)
    parts = jnp.where(lane == 0, high, jnp.where(lane == 1, middle, low))
    kept = (lane < 3) & (lax.broadcasted_iota(jnp.int32, shape, 0) == 0)
    out_ref[nb:, :] = jnp.where(kept, parts, 0.0).astype(out_ref.dtype)


def pieces_kernel(yh_ref, freq_ref, both_ref, out_ref, turned_ref):
    sub = out_ref.shape[1]
    nb = out_ref.shape[2] // YH
    step = jnp.full((1, 128), freq_ref[0], jnp.int32).astype(jnp.float32)
    omega = 0.1 * jnp.exp(math.log(20.0) * step / (NFREQ - 1))
    scaled = []
    for i in range(YH):
        label = both_ref[i, nb:, :128].astype(jnp.float32)
        energy = jnp.sum(jnp.sum(label, axis=1, keepdims=True), axis=0, keepdims=True)
        coef = energy / (energy * energy + omega * omega)
        scaled.append(both_ref[i, :nb, :].astype(jnp.float32) * coef[:, :1])
    turned_ref[...] = jnp.concatenate(scaled, axis=0).T.astype(turned_ref.dtype)
    for z in range(Z):
        start = pl.multiple_of((z * YH + yh_ref[0]) * sub, sub)
        out_ref[z] = turned_ref[pl.ds(start, sub), :]


def rows_kernel(got_ref, out_ref):
    out_ref[...] = jnp.concatenate([got_ref[z] for z in range(Z)], axis=1)


def proj_kernel(wt_ref, *refs):
    row_refs, out_ref = refs[:-1], refs[-1]
    tile = GROUP * (out_ref.shape[1] // (Z * YH))
    for g in range(out_ref.shape[1] // tile):
        span = slice(g * tile, (g + 1) * tile)
        rows = jnp.concatenate([r[:, span] for r in row_refs], axis=0)
        out_ref[:, span] = jnp.dot(
            wt_ref[...], rows, preferred_element_type=jnp.float32
        ).astype(out_ref.dtype)


def sigma_kernel(cols_ref, proj_ref, out_ref, cols_buf, proj_buf, sems):
    groups, count, sides, nb, width = cols_buf.shape
    tile = count * sides * nb
    copies = [
        (
            pltpu.make_async_copy(
                cols_ref.at[pl.ds(g * count, count), :, pl.ds(0, nb)], cols_buf.at[g], sems.at[g, 0]
            ),
            pltpu.make_async_copy(proj_ref.at[:, pl.ds(g * tile, tile)], proj_buf.at[g], sems.at[g, 1]),
        )
        for g in range(groups)
    ]
    for copy in sum(copies, ()):
        copy.start()
    sigma = jnp.zeros((nb, nb), jnp.float32)
    for g in range(groups):
        for copy in copies[g]:
            copy.wait()
        block = jnp.dot(
            cols_buf[g].reshape(tile, width), proj_buf[g], preferred_element_type=jnp.float32
        )
        for i in range(GROUP):
            sigma += block[i * nb : (i + 1) * nb, i * nb : (i + 1) * nb]
    out_ref[...] = sigma.T


def on_device(pair_dens, energies, freq_index, screened):
    mine = pair_dens[0]
    nb, width = mine.shape
    sub = width // (Z * YH)
    rowcount = X * YL * CORE * sub
    mcols = Z * YH * nb
    tile = GROUP * nb
    place = {axis: lax.axis_index(axis).astype(jnp.int32).reshape(1) for axis in ("yh", "x", "core")}
    swap = [(0, 1), (1, 0)]

    labelled = pl.pallas_call(
        label_kernel,
        out_shape=jax.ShapeDtypeStruct((nb + 8, width), jnp.bfloat16),
        in_specs=[SMEM, VMEM],
        out_specs=VMEM,
        compiler_params=PARAMS,
    )(energies, mine)
    both = lax.optimization_barrier(lax.all_gather(labelled, "yh"))
    cols = lax.all_gather(both, "z")

    pieces = pl.pallas_call(
        pieces_kernel,
        out_shape=jax.ShapeDtypeStruct((Z, sub, YH * nb), jnp.bfloat16),
        in_specs=[SMEM, SMEM, VMEM],
        out_specs=VMEM,
        scratch_shapes=[pltpu.VMEM((width, YH * nb), jnp.bfloat16)],
        compiler_params=PARAMS,
    )(place["yh"], freq_index, both)
    got = lax.all_to_all(pieces, "z", 0, 0, tiled=True)
    rows = pl.pallas_call(
        rows_kernel,
        out_shape=jax.ShapeDtypeStruct((sub, mcols), jnp.bfloat16),
        in_specs=[VMEM],
        out_specs=VMEM,
        compiler_params=PARAMS,
    )(got)
    rows = lax.all_gather(rows, "yl", axis=0, tiled=True)
    turned = pl.pallas_call(
        turn_kernel,
        out_shape=jax.ShapeDtypeStruct((width, rowcount), jnp.bfloat16),
        in_specs=[SMEM, SMEM, pl.BlockSpec(memory_space=pl.ANY), VMEM],
        out_specs=VMEM,
        compiler_params=PARAMS,
        cost_estimate=pl.CostEstimate(flops=0, bytes_accessed=4 * rowcount * width, transcendentals=0),
    )(place["x"], place["core"], rows, screened[0])
    further = [
        lax.ppermute(rows, "x", [(i, (i - step) % X) for i in range(X)]) for step in range(1, X)
    ]
    further[0], turned = lax.optimization_barrier((further[0], turned))
    blocks = []
    for block in [rows] + further:
        blocks += [block, lax.ppermute(block, "core", swap)]

    proj = pl.pallas_call(
        proj_kernel,
        out_shape=jax.ShapeDtypeStruct((width, mcols), jnp.bfloat16),
        in_specs=[VMEM] * (1 + len(blocks)),
        out_specs=VMEM,
        compiler_params=PARAMS,
        cost_estimate=pl.CostEstimate(
            flops=2 * width * mcols * rowcount, bytes_accessed=10 << 20, transcendentals=0
        ),
    )(turned, *blocks)
    part = pl.pallas_call(
        sigma_kernel,
        out_shape=jax.ShapeDtypeStruct((nb, nb), jnp.float32),
        in_specs=[pl.BlockSpec(memory_space=pl.ANY)] * 2,
        out_specs=VMEM,
        scratch_shapes=[
            pltpu.VMEM((mcols // tile, GROUP // YH, YH, nb, width), jnp.bfloat16),
            pltpu.VMEM((mcols // tile, width, tile), jnp.bfloat16),
            pltpu.SemaphoreType.DMA((mcols // tile, 2)),
        ],
        compiler_params=pltpu.CompilerParams(vmem_limit_bytes=60 << 20),
        cost_estimate=pl.CostEstimate(
            flops=2 * width * mcols * tile, bytes_accessed=6 << 20, transcendentals=0
        ),
    )(cols, proj)

    share = nb // (Z * YH)
    part = lax.all_to_all(part.reshape(Z * YH, share, nb), BAND, 0, 0, tiled=True).sum(axis=0)
    spread = jnp.broadcast_to(part[None], (X * YL * CORE, share, nb))
    return lax.all_to_all(spread, GA, 0, 0, tiled=True).sum(axis=0)


def solution(mesh):
    fine = Mesh(mesh.devices.reshape(Z, YH, X, YL, CORE), BAND + GA)
    return jax.shard_map(
        on_device,
        mesh=fine,
        in_specs=(P(BAND, None, GA), P(BAND), P(), P(BAND, None, None, GA)),
        out_specs=P(BAND, None),
        check_vma=False,
    )
```

time: 152 us -> 150 us (0.987)
  blocking collectives: 45.9 us -> 87.5 us
  starting transfers between devices: 56.8 us -> 28.2 us
  waiting for transfers between devices: 15 us -> 1.71 us
  other arithmetic: 2.27 us -> 0.64 us
    all_to_all x0 -> x1, blocking collectives: none -> 23.9 us  [on_device(): got = lax.all_to_all(pieces, 'z', 0, 0, tiled=True)]
    all_to_all x1 -> x0, starting transfers between devices: 14.9 us -> none  [on_device(): got = lax.all_to_all(pieces, 'z', 0, 0, tiled=True)]
    all_gather x0 -> x1, blocking collectives: none -> 11.7 us  [on_device(): both = lax.optimization_barrier(lax.all_gather(labelled, 'yh'))]
    ppermute x2 -> x0, starting transfers between devices: 10.2 us -> none  [the longest x1 8.27 us: on_device(): theirs = lax.ppermute(mine, 'yh', swap)]
    all_to_all x1 -> x0, waiting for transfers between devices: 9.11 us -> none  [on_device(): got = lax.all_to_all(pieces, 'z', 0, 0, tiled=True)]
    all_gather x1, blocking collectives: 12.4 us -> 17.5 us  [on_device(): rows = lax.all_gather(rows, 'yl', axis=0, tiled=True)]
    ppermute x2 -> x0, waiting for transfers between devices: 4.46 us -> none  [the longest x1 4.45 us: on_device(): lax.ppermute(give, 'yh', swap)]
    ppermute x4, starting transfers between devices: 22.3 us -> 19 us  [on_device(): blocks += [block, lax.ppermute(block, 'core', swap)]]
  transfers between devices with their start and end apart: 11 -> 8, of which waited for: 3 -> 2; matrix products, arithmetic and copies ran while one was open for 1% -> 0% of each run, Pallas kernels for 5% -> 5%
where the time goes in v4:
time: 150 us
  blocking collectives  87.5 us (58%)
  starting transfers between devices  28.2 us (19%)
  between operations  14.9 us (10%)
  Pallas kernels  11.4 us (8%)
  local copies, waits for them, and re-layouts  5.4 us (4%)
  waiting for transfers between devices  1.71 us (1%)
    all_to_all x1, blocking collectives, on_device(): got = lax.all_to_all(pieces, 'z', 0, 0, tiled=True)  23.9 us
    ppermute x4, starting transfers between devices, on_device(): blocks += [block, lax.ppermute(block, 'core', swap)]  19 us
    all_to_all x1, blocking collectives, on_device(): lax.all_to_all(part.reshape(Z * YH, share, nb), BAND, 0, 0, tiled=True)  18.3 us
    all_gather x1, blocking collectives, on_device(): rows = lax.all_gather(rows, 'yl', axis=0, tiled=True)  17.5 us
    all_to_all x1, blocking collectives, on_device(): return lax.all_to_all(spread, GA, 0, 0, tiled=True).sum(axis=0)  16.2 us
    all_gather x1, blocking collectives, on_device(): both = lax.optimization_barrier(lax.all_gather(labelled, 'yh'))  11.7 us
    ppermute x3, starting transfers between devices, on_device(): lax.ppermute(rows, 'x', [(i, (i - step) % X) for i in range(X)])  9.21 us
    pallas_call x1, Pallas kernels, on_device(): pl.pallas_call(proj_kernel, out_shape=jax.ShapeDtypeStruct((width, mcols)...  5.66 us
  transfers between devices with their start and end apart: 8, of which 2 were waited for; matrix products, arithmetic and copies ran while one was open for 0% of the time, Pallas kernels for 5%

profile of v4, /device:TPU:1, one launch (start us, length us, event | category | flops | bytes accessed | tf_op | source)
XLA Modules:
  0.0 149.8 jit_solution(11441229805607798412)
XLA Ops:
  6.5 0.0 all-gather.4.cloned.1.call-start
  7.2 0.0 copy-start.3
  7.2 0.9 copy-done.3
  8.1 11.7 %all-gather = bf16[112,1152]{1,0:T(8,128)(2,1)} all-gather(bf16[56,1152]{1,0:T(8,128)(2,1)S(1)} %shard_map.46), channel_id=2, replica_groups=mesh['z'=12,'yh'=2,'x'=4,'yl'=4,'core'=2] {'yh'}, dimensions={0}, use_global_device_ids=true | all-gather | bytes 387072 | tf_op jit(solution)/shard_map/all_gather | solution.py:120
  19.8 0.0 all-gather.4.cloned.1.call-update
  20.5 0.0 copy-start.2
  20.5 0.9 copy-done.2
  21.5 0.3 shard_map.47
  21.7 23.9 %all_to_all.15.got_ref = bf16[12,48,96]{2,1,0:T(8,128)(2,1)S(1)} all-to-all(bf16[12,48,96]{2,1,0:T(8,128)(2,1)S(1)} %shard_map.47), channel_id=1, replica_groups=mesh['z'=12,'yh'=2,'x'=4,'yl'=4,'core'=2] {'z'}, dimensions={0} | all-to-all | bytes 221184 | tf_op jit(solution)/shard_map/all_to_all | solution.py:131
  45.6 0.1 shard_map.48
  45.7 17.5 %all_gather.19._.refs_0_ = bf16[192,1152]{1,0:T(8,128)(2,1)S(1)} all-gather(bf16[48,1152]{1,0:T(8,128)(2,1)S(1)} %shard_map.48), channel_id=1, replica_groups=mesh['z'=12,'yh'=2,'x'=4,'yl'=4,'core'=2] {'yl'}, dimensions={0}, use_global_device_ids=true | all-gather | bytes 552960 | tf_op jit(solution)/shard_map/all_gather | solution.py:139
  63.2 4.3 %collective-permute-start = (bf16[192,1152]{1,0:T(8,128)(2,1)S(1)}, bf16[192,1152]{1,0:T(8,128)(2,1)S(1)}, u32[]{:S(2)}, u32[]{:S(2)}) collective-permute-start(bf16[192,1152]{1,0:T(8,128)(2,1)S(1)} %all_gather.19._.refs_0_), channel_id=1, source_target_pairs={{0,24},{8,0},{16,8},{24,16},{1,25},{9,1},{17,9},{25,17},{2,26},{10... | collective-permute-start | bytes 1327112 | tf_op jit(solution)/shard_map/ppermute | solution.py:149
  67.5 2.5 %collective-permute-start.3 = (bf16[192,1152]{1,0:T(8,128)(2,1)S(1)}, bf16[192,1152]{1,0:T(8,128)(2,1)S(1)}, u32[]{:S(2)}, u32[]{:S(2)}) collective-permute-start(bf16[192,1152]{1,0:T(8,128)(2,1)S(1)} %all_gather.19._.refs_0_), channel_id=1, source_target_pairs={{0,16},{8,24},{16,0},{24,8},{1,17},{9,25},{17,1},{25,9},{2,18},{10... | collective-permute-start | bytes 1327112 | tf_op jit(solution)/shard_map/ppermute | solution.py:149
  70.0 2.4 %collective-permute-start.5 = (bf16[192,1152]{1,0:T(8,128)(2,1)S(1)}, bf16[192,1152]{1,0:T(8,128)(2,1)S(1)}, u32[]{:S(2)}, u32[]{:S(2)}) collective-permute-start(bf16[192,1152]{1,0:T(8,128)(2,1)S(1)} %all_gather.19._.refs_0_), channel_id=1, source_target_pairs={{0,8},{8,16},{16,24},{24,0},{1,9},{9,17},{17,25},{25,1},{2,10},{10... | collective-permute-start | bytes 1327112 | tf_op jit(solution)/shard_map/ppermute | solution.py:149
  72.5 6.5 %collective-permute-start.1 = (bf16[192,1152]{1,0:T(8,128)(2,1)S(1)}, bf16[192,1152]{1,0:T(8,128)(2,1)S(1)}, u32[]{:S(2)}, u32[]{:S(2)}) collective-permute-start(bf16[192,1152]{1,0:T(8,128)(2,1)S(1)} %all_gather.19._.refs_0_), channel_id=1, source_target_pairs={{0,1},{1,0},{2,3},{3,2},{4,5},{5,4},{6,7},{7,6},{8,9},{9,8},{10,11... | collective-permute-start | bytes 1327112 | tf_op jit(solution)/shard_map/ppermute | solution.py:154
  78.9 0.0 copy-start
  78.9 2.0 %copy-done = bf16[1,32,48,1152]{3,2,1,0:T(8,128)(2,1)S(1)} copy-done((bf16[1,32,48,1152]{3,2,1,0:T(8,128)(2,1)S(1)}, bf16[1,32,48,1152]{3,2,1,0:T(8,128)(2,1)}, u32[]{:S(2)}) %copy-start) | copy-done | bytes 3538968
  81.0 1.0 shard_map.49.wt_ref
  81.9 0.0 collective-permute-done.refs_2_
  81.9 7.3 %collective-permute-start.2 = (bf16[192,1152]{1,0:T(8,128)(2,1)S(1)}, bf16[192,1152]{1,0:T(8,128)(2,1)S(1)}, u32[]{:S(2)}, u32[]{:S(2)}) collective-permute-start(bf16[192,1152]{1,0:T(8,128)(2,1)S(1)} %collective-permute-done.refs_2_), channel_id=1, source_target_pairs={{0,1},{1,0},{2,3},{3,2},{4,5},{5,4},{6,7},{7,6},{8,9},{9,8},{10,11... | collective-permute-start | bytes 1327112 | tf_op jit(solution)/shard_map/ppermute | solution.py:154
  89.3 0.0 collective-permute-done.3.refs_4_
  89.3 1.9 %collective-permute-start.4 = (bf16[192,1152]{1,0:T(8,128)(2,1)S(1)}, bf16[192,1152]{1,0:T(8,128)(2,1)S(1)}, u32[]{:S(2)}, u32[]{:S(2)}) collective-permute-start(bf16[192,1152]{1,0:T(8,128)(2,1)S(1)} %collective-permute-done.3.refs_4_), channel_id=1, source_target_pairs={{0,1},{1,0},{2,3},{3,2},{4,5},{5,4},{6,7},{7,6},{8,9},{9,8},{10,11... | collective-permute-start | bytes 1327112 | tf_op jit(solution)/shard_map/ppermute | solution.py:154
  91.2 0.3 collective-permute-done.5.refs_6_
  91.5 3.3 %collective-permute-start.6 = (bf16[192,1152]{1,0:T(8,128)(2,1)S(1)}, bf16[192,1152]{1,0:T(8,128)(2,1)S(1)}, u32[]{:S(2)}, u32[]{:S(2)}) collective-permute-start(bf16[192,1152]{1,0:T(8,128)(2,1)S(1)} %collective-permute-done.5.refs_6_), channel_id=1, source_target_pairs={{0,1},{1,0},{2,3},{3,2},{4,5},{5,4},{6,7},{7,6},{8,9},{9,8},{10,11... | collective-permute-start | bytes 1327112 | tf_op jit(solution)/shard_map/ppermute | solution.py:154
  94.9 0.0 collective-permute-done.1.refs_1_
  94.9 0.0 collective-permute-done.2.refs_3_
  94.9 0.0 collective-permute-done.4.refs_5_
  94.9 1.4 collective-permute-done.6.refs_7_
  96.3 5.7 %shard_map.50.proj_ref = bf16[1152,1152]{1,0:T(8,128)(2,1)S(1)} custom-call(bf16[1152,1536]{1,0:T(8,128)(2,1)S(1)} %shard_map.49.wt_ref, bf16[192,1152]{1,0:T(8,128)(2,1)S(1)} %all_gather.19._.refs_0_, bf16[192,1152]{1,0:T(8,128)(2,1)S(1)} %collective-permute-done.1.refs_1_, bf16[192,1152]{1,0:T(8,128)(2,1)S(1)} %collective-permute-done.refs_2_, ...), custom_call_target="tpu_custom_call" | custom-call | flops 4076863488 | bytes 10485760 | tf_op jit(solution)/shard_map/pallas_call | solution.py:156
  101.9 0.0 copy-start.1
  101.9 1.5 %copy-done.1 = bf16[1152,1152]{1,0:T(8,128)(2,1)} copy-done((bf16[1152,1152]{1,0:T(8,128)(2,1)}, bf16[1152,1152]{1,0:T(8,128)(2,1)S(1)}, u32[]{:S(2)}) %copy-start.1) | copy-done | bytes 2654232
  103.5 0.0 all-gather.4.cloned.1.call-done
  103.5 4.3 %shard_map.51 = f32[48,48]{1,0:T(8,128)} custom-call(bf16[12,2,56,1152]{3,2,1,0:T(8,128)(2,1)} %bitcast.12, bf16[1152,1152]{1,0:T(8,128)(2,1)} %copy-done.1), custom_call_target="tpu_custom_call" | custom-call | flops 1019215872 | bytes 6291456 | tf_op jit(solution)/shard_map/pallas_call | solution.py:166
  107.8 18.3 %all_to_all.16 = f32[24,2,48]{2,1,0:T(2,128)S(1)} all-to-all(f32[24,2,48]{2,1,0:T(2,128)} %bitcast.13), channel_id=1, replica_groups=mesh['z'=12,'yh'=2,'x'=4,'yl'=4,'core'=2] {'z','yh'}, dimensions={0} | all-to-all | bytes 18432 | tf_op jit(solution)/shard_map/all_to_all | solution.py:183
  126.1 16.2 %all_to_all.17 = f32[32,2,48]{2,1,0:T(2,128)S(1)} all-to-all(f32[32,2,48]{2,1,0:T(2,128)S(1)} %broadcast_in_dim.2), channel_id=1, replica_groups=mesh['z'=12,'yh'=2,'x'=4,'yl'=4,'core'=2] {'x','yl','core'}, dimensions={0} | all-to-all | bytes 24576 | tf_op jit(solution)/shard_map/all_to_all | solution.py:185
  142.3 0.6 reduce_sum.19
  (3 shorter events, 0.1 us)
Async XLA Ops:
  6.5 96.9 %all-gather.4.cloned.1.call-start = ((), (), s32[]{:S(2)}) async-start(), calls=%async_computation.3 | async-start | bytes 3354624 | tf_op jit(solution)/shard_map/all_gather | solution.py:121
  7.2 0.9 copy-start.3
  20.5 0.9 copy-start.2
  63.2 18.7 %collective-permute-start = (bf16[192,1152]{1,0:T(8,128)(2,1)S(1)}, bf16[192,1152]{1,0:T(8,128)(2,1)S(1)}, u32[]{:S(2)}, u32[]{:S(2)}) collective-permute-start(bf16[192,1152]{1,0:T(8,128)(2,1)S(1)} %all_gather.19._.refs_0_), channel_id=1, source_target_pairs={{0,24},{8,0},{16,8},{24,16},{1,25},{9,1},{17,9},{25,17},{2,26},{10... | collective-permute-start | bytes 1327112 | tf_op jit(solution)/shard_map/ppermute | solution.py:149
  67.5 21.8 %collective-permute-start.3 = (bf16[192,1152]{1,0:T(8,128)(2,1)S(1)}, bf16[192,1152]{1,0:T(8,128)(2,1)S(1)}, u32[]{:S(2)}, u32[]{:S(2)}) collective-permute-start(bf16[192,1152]{1,0:T(8,128)(2,1)S(1)} %all_gather.19._.refs_0_), channel_id=1, source_target_pairs={{0,16},{8,24},{16,0},{24,8},{1,17},{9,25},{17,1},{25,9},{2,18},{10... | collective-permute-start | bytes 1327112 | tf_op jit(solution)/shard_map/ppermute | solution.py:149
  70.0 21.5 %collective-permute-start.5 = (bf16[192,1152]{1,0:T(8,128)(2,1)S(1)}, bf16[192,1152]{1,0:T(8,128)(2,1)S(1)}, u32[]{:S(2)}, u32[]{:S(2)}) collective-permute-start(bf16[192,1152]{1,0:T(8,128)(2,1)S(1)} %all_gather.19._.refs_0_), channel_id=1, source_target_pairs={{0,8},{8,16},{16,24},{24,0},{1,9},{9,17},{17,25},{25,1},{2,10},{10... | collective-permute-start | bytes 1327112 | tf_op jit(solution)/shard_map/ppermute | solution.py:149
  72.5 22.4 %collective-permute-start.1 = (bf16[192,1152]{1,0:T(8,128)(2,1)S(1)}, bf16[192,1152]{1,0:T(8,128)(2,1)S(1)}, u32[]{:S(2)}, u32[]{:S(2)}) collective-permute-start(bf16[192,1152]{1,0:T(8,128)(2,1)S(1)} %all_gather.19._.refs_0_), channel_id=1, source_target_pairs={{0,1},{1,0},{2,3},{3,2},{4,5},{5,4},{6,7},{7,6},{8,9},{9,8},{10,11... | collective-permute-start | bytes 1327112 | tf_op jit(solution)/shard_map/ppermute | solution.py:154
  78.9 2.0 %copy-start = (bf16[1,32,48,1152]{3,2,1,0:T(8,128)(2,1)S(1)}, bf16[1,32,48,1152]{3,2,1,0:T(8,128)(2,1)}, u32[]{:S(2)}) copy-start(bf16[1,32,48,1152]{3,2,1,0:T(8,128)(2,1)} %param.7) | copy-start | bytes 10616836
  81.9 12.9 %collective-permute-start.2 = (bf16[192,1152]{1,0:T(8,128)(2,1)S(1)}, bf16[192,1152]{1,0:T(8,128)(2,1)S(1)}, u32[]{:S(2)}, u32[]{:S(2)}) collective-permute-start(bf16[192,1152]{1,0:T(8,128)(2,1)S(1)} %collective-permute-done.refs_2_), channel_id=1, source_target_pairs={{0,1},{1,0},{2,3},{3,2},{4,5},{5,4},{6,7},{7,6},{8,9},{9,8},{10,11... | collective-permute-start | bytes 1327112 | tf_op jit(solution)/shard_map/ppermute | solution.py:154
  89.3 5.6 %collective-permute-start.4 = (bf16[192,1152]{1,0:T(8,128)(2,1)S(1)}, bf16[192,1152]{1,0:T(8,128)(2,1)S(1)}, u32[]{:S(2)}, u32[]{:S(2)}) collective-permute-start(bf16[192,1152]{1,0:T(8,128)(2,1)S(1)} %collective-permute-done.3.refs_4_), channel_id=1, source_target_pairs={{0,1},{1,0},{2,3},{3,2},{4,5},{5,4},{6,7},{7,6},{8,9},{9,8},{10,11... | collective-permute-start | bytes 1327112 | tf_op jit(solution)/shard_map/ppermute | solution.py:154
  91.5 4.7 %collective-permute-start.6 = (bf16[192,1152]{1,0:T(8,128)(2,1)S(1)}, bf16[192,1152]{1,0:T(8,128)(2,1)S(1)}, u32[]{:S(2)}, u32[]{:S(2)}) collective-permute-start(bf16[192,1152]{1,0:T(8,128)(2,1)S(1)} %collective-permute-done.5.refs_6_), channel_id=1, source_target_pairs={{0,1},{1,0},{2,3},{3,2},{4,5},{5,4},{6,7},{7,6},{8,9},{9,8},{10,11... | collective-permute-start | bytes 1327112 | tf_op jit(solution)/shard_map/ppermute | solution.py:154
  101.9 1.5 %copy-start.1 = (bf16[1152,1152]{1,0:T(8,128)(2,1)}, bf16[1152,1152]{1,0:T(8,128)(2,1)S(1)}, u32[]{:S(2)}) copy-start(bf16[1152,1152]{1,0:T(8,128)(2,1)S(1)} %shard_map.50.proj_ref) | copy-start | bytes 7962628
Sparse Core Ops, SparseCore 0:
  20.0 66.2 all-gather.3

commit v5 on v4

--- a/solution.py
+++ b/solution.py
@@ -13,6 +13,7 @@
 BAND = ("z", "yh")
 GA = ("x", "yl", "core")
 GROUP = 8
+SPANS = [slice(i, min(i + 256, 1152)) for i in range(0, 1152, 256)]
 VMEM = pl.BlockSpec(memory_space=pltpu.VMEM)
 SMEM = pl.BlockSpec(memory_space=pltpu.SMEM)
 PARAMS = pltpu.CompilerParams(vmem_limit_bytes=16 << 20)
@@ -65,9 +66,7 @@
 
 def proj_kernel(wt_ref, *refs):
     row_refs, out_ref = refs[:-1], refs[-1]
-    tile = GROUP * (out_ref.shape[1] // (Z * YH))
-    for g in range(out_ref.shape[1] // tile):
-        span = slice(g * tile, (g + 1) * tile)
+    for span in SPANS:
         rows = jnp.concatenate([r[:, span] for r in row_refs], axis=0)
         out_ref[:, span] = jnp.dot(
             wt_ref[...], rows, preferred_element_type=jnp.float32

time: 150 us -> 149 us (level)
  transfers between devices with their start and end apart: 8 -> 8, of which waited for: 2 -> 2; matrix products, arithmetic and copies ran while one was open for 0% -> 0% of each run, Pallas kernels for 5% -> 4%
where the time goes in v5:
time: 149 us
  blocking collectives  87.5 us (59%)
  starting transfers between devices  28.2 us (19%)
  between operations  14.9 us (10%)
  Pallas kernels  10.4 us (7%)
  local copies, waits for them, and re-layouts  5.4 us (4%)
  waiting for transfers between devices  1.71 us (1%)
    all_to_all x1, blocking collectives, on_device(): got = lax.all_to_all(pieces, 'z', 0, 0, tiled=True)  23.9 us
    ppermute x4, starting transfers between devices, on_device(): blocks += [block, lax.ppermute(block, 'core', swap)]  19 us
    all_to_all x1, blocking collectives, on_device(): lax.all_to_all(part.reshape(Z * YH, share, nb), BAND, 0, 0, tiled=True)  18.3 us
    all_gather x1, blocking collectives, on_device(): rows = lax.all_gather(rows, 'yl', axis=0, tiled=True)  17.5 us
    all_to_all x1, blocking collectives, on_device(): return lax.all_to_all(spread, GA, 0, 0, tiled=True).sum(axis=0)  16.2 us
    all_gather x1, blocking collectives, on_device(): both = lax.optimization_barrier(lax.all_gather(labelled, 'yh'))  11.7 us
    ppermute x3, starting transfers between devices, on_device(): lax.ppermute(rows, 'x', [(i, (i - step) % X) for i in range(X)])  9.21 us
    unnamed x8, local copies, waits for them, and re-layouts  5.38 us
  transfers between devices with their start and end apart: 8, of which 2 were waited for; matrix products, arithmetic and copies ran while one was open for 0% of the time, Pallas kernels for 4%

profile of v5, /device:TPU:1, one launch (start us, length us, event | category | flops | bytes accessed | tf_op | source)
XLA Modules:
  0.0 148.8 jit_solution(7127923682407884959)
XLA Ops:
  6.5 0.0 all-gather.4.cloned.1.call-start
  7.2 0.0 copy-start.3
  7.2 0.9 copy-done.3
  8.1 11.7 %all-gather = bf16[112,1152]{1,0:T(8,128)(2,1)} all-gather(bf16[56,1152]{1,0:T(8,128)(2,1)S(1)} %shard_map.46), channel_id=2, replica_groups=mesh['z'=12,'yh'=2,'x'=4,'yl'=4,'core'=2] {'yh'}, dimensions={0}, use_global_device_ids=true | all-gather | bytes 387072 | tf_op jit(solution)/shard_map/all_gather | solution.py:119
  19.8 0.0 all-gather.4.cloned.1.call-update
  20.5 0.0 copy-start.2
  20.5 0.9 copy-done.2
  21.5 0.3 shard_map.47
  21.7 23.9 %all_to_all.15.got_ref = bf16[12,48,96]{2,1,0:T(8,128)(2,1)S(1)} all-to-all(bf16[12,48,96]{2,1,0:T(8,128)(2,1)S(1)} %shard_map.47), channel_id=1, replica_groups=mesh['z'=12,'yh'=2,'x'=4,'yl'=4,'core'=2] {'z'}, dimensions={0} | all-to-all | bytes 221184 | tf_op jit(solution)/shard_map/all_to_all | solution.py:130
  45.6 0.1 shard_map.48
  45.7 17.5 %all_gather.19._.refs_0_ = bf16[192,1152]{1,0:T(8,128)(2,1)S(1)} all-gather(bf16[48,1152]{1,0:T(8,128)(2,1)S(1)} %shard_map.48), channel_id=1, replica_groups=mesh['z'=12,'yh'=2,'x'=4,'yl'=4,'core'=2] {'yl'}, dimensions={0}, use_global_device_ids=true | all-gather | bytes 552960 | tf_op jit(solution)/shard_map/all_gather | solution.py:138
  63.2 4.3 %collective-permute-start = (bf16[192,1152]{1,0:T(8,128)(2,1)S(1)}, bf16[192,1152]{1,0:T(8,128)(2,1)S(1)}, u32[]{:S(2)}, u32[]{:S(2)}) collective-permute-start(bf16[192,1152]{1,0:T(8,128)(2,1)S(1)} %all_gather.19._.refs_0_), channel_id=1, source_target_pairs={{0,24},{8,0},{16,8},{24,16},{1,25},{9,1},{17,9},{25,17},{2,26},{10... | collective-permute-start | bytes 1327112 | tf_op jit(solution)/shard_map/ppermute | solution.py:148
  67.5 2.5 %collective-permute-start.3 = (bf16[192,1152]{1,0:T(8,128)(2,1)S(1)}, bf16[192,1152]{1,0:T(8,128)(2,1)S(1)}, u32[]{:S(2)}, u32[]{:S(2)}) collective-permute-start(bf16[192,1152]{1,0:T(8,128)(2,1)S(1)} %all_gather.19._.refs_0_), channel_id=1, source_target_pairs={{0,16},{8,24},{16,0},{24,8},{1,17},{9,25},{17,1},{25,9},{2,18},{10... | collective-permute-start | bytes 1327112 | tf_op jit(solution)/shard_map/ppermute | solution.py:148
  70.0 2.4 %collective-permute-start.5 = (bf16[192,1152]{1,0:T(8,128)(2,1)S(1)}, bf16[192,1152]{1,0:T(8,128)(2,1)S(1)}, u32[]{:S(2)}, u32[]{:S(2)}) collective-permute-start(bf16[192,1152]{1,0:T(8,128)(2,1)S(1)} %all_gather.19._.refs_0_), channel_id=1, source_target_pairs={{0,8},{8,16},{16,24},{24,0},{1,9},{9,17},{17,25},{25,1},{2,10},{10... | collective-permute-start | bytes 1327112 | tf_op jit(solution)/shard_map/ppermute | solution.py:148
  72.5 6.5 %collective-permute-start.1 = (bf16[192,1152]{1,0:T(8,128)(2,1)S(1)}, bf16[192,1152]{1,0:T(8,128)(2,1)S(1)}, u32[]{:S(2)}, u32[]{:S(2)}) collective-permute-start(bf16[192,1152]{1,0:T(8,128)(2,1)S(1)} %all_gather.19._.refs_0_), channel_id=1, source_target_pairs={{0,1},{1,0},{2,3},{3,2},{4,5},{5,4},{6,7},{7,6},{8,9},{9,8},{10,11... | collective-permute-start | bytes 1327112 | tf_op jit(solution)/shard_map/ppermute | solution.py:153
  78.9 0.0 copy-start
  78.9 2.0 %copy-done = bf16[1,32,48,1152]{3,2,1,0:T(8,128)(2,1)S(1)} copy-done((bf16[1,32,48,1152]{3,2,1,0:T(8,128)(2,1)S(1)}, bf16[1,32,48,1152]{3,2,1,0:T(8,128)(2,1)}, u32[]{:S(2)}) %copy-start) | copy-done | bytes 3538968
  81.0 1.0 shard_map.49.wt_ref
  81.9 0.0 collective-permute-done.refs_2_
  81.9 7.3 %collective-permute-start.2 = (bf16[192,1152]{1,0:T(8,128)(2,1)S(1)}, bf16[192,1152]{1,0:T(8,128)(2,1)S(1)}, u32[]{:S(2)}, u32[]{:S(2)}) collective-permute-start(bf16[192,1152]{1,0:T(8,128)(2,1)S(1)} %collective-permute-done.refs_2_), channel_id=1, source_target_pairs={{0,1},{1,0},{2,3},{3,2},{4,5},{5,4},{6,7},{7,6},{8,9},{9,8},{10,11... | collective-permute-start | bytes 1327112 | tf_op jit(solution)/shard_map/ppermute | solution.py:153
  89.3 0.0 collective-permute-done.3.refs_4_
  89.3 1.9 %collective-permute-start.4 = (bf16[192,1152]{1,0:T(8,128)(2,1)S(1)}, bf16[192,1152]{1,0:T(8,128)(2,1)S(1)}, u32[]{:S(2)}, u32[]{:S(2)}) collective-permute-start(bf16[192,1152]{1,0:T(8,128)(2,1)S(1)} %collective-permute-done.3.refs_4_), channel_id=1, source_target_pairs={{0,1},{1,0},{2,3},{3,2},{4,5},{5,4},{6,7},{7,6},{8,9},{9,8},{10,11... | collective-permute-start | bytes 1327112 | tf_op jit(solution)/shard_map/ppermute | solution.py:153
  91.2 0.3 collective-permute-done.5.refs_6_
  91.5 3.3 %collective-permute-start.6 = (bf16[192,1152]{1,0:T(8,128)(2,1)S(1)}, bf16[192,1152]{1,0:T(8,128)(2,1)S(1)}, u32[]{:S(2)}, u32[]{:S(2)}) collective-permute-start(bf16[192,1152]{1,0:T(8,128)(2,1)S(1)} %collective-permute-done.5.refs_6_), channel_id=1, source_target_pairs={{0,1},{1,0},{2,3},{3,2},{4,5},{5,4},{6,7},{7,6},{8,9},{9,8},{10,11... | collective-permute-start | bytes 1327112 | tf_op jit(solution)/shard_map/ppermute | solution.py:153
  94.9 0.0 collective-permute-done.1.refs_1_
  94.9 0.0 collective-permute-done.2.refs_3_
  94.9 0.0 collective-permute-done.4.refs_5_
  94.9 1.4 collective-permute-done.6.refs_7_
  96.3 4.8 %shard_map.50.proj_ref = bf16[1152,1152]{1,0:T(8,128)(2,1)S(1)} custom-call(bf16[1152,1536]{1,0:T(8,128)(2,1)S(1)} %shard_map.49.wt_ref, bf16[192,1152]{1,0:T(8,128)(2,1)S(1)} %all_gather.19._.refs_0_, bf16[192,1152]{1,0:T(8,128)(2,1)S(1)} %collective-permute-done.1.refs_1_, bf16[192,1152]{1,0:T(8,128)(2,1)S(1)} %collective-permute-done.refs_2_, ...), custom_call_target="tpu_custom_call" | custom-call | flops 4076863488 | bytes 10485760 | tf_op jit(solution)/shard_map/pallas_call | solution.py:155
  101.0 0.0 copy-start.1
  101.0 1.5 %copy-done.1 = bf16[1152,1152]{1,0:T(8,128)(2,1)} copy-done((bf16[1152,1152]{1,0:T(8,128)(2,1)}, bf16[1152,1152]{1,0:T(8,128)(2,1)S(1)}, u32[]{:S(2)}) %copy-start.1) | copy-done | bytes 2654232
  102.6 0.0 all-gather.4.cloned.1.call-done
  102.6 4.3 %shard_map.51 = f32[48,48]{1,0:T(8,128)} custom-call(bf16[12,2,56,1152]{3,2,1,0:T(8,128)(2,1)} %bitcast.12, bf16[1152,1152]{1,0:T(8,128)(2,1)} %copy-done.1), custom_call_target="tpu_custom_call" | custom-call | flops 1019215872 | bytes 6291456 | tf_op jit(solution)/shard_map/pallas_call | solution.py:165
  106.9 18.3 %all_to_all.16 = f32[24,2,48]{2,1,0:T(2,128)S(1)} all-to-all(f32[24,2,48]{2,1,0:T(2,128)} %bitcast.13), channel_id=1, replica_groups=mesh['z'=12,'yh'=2,'x'=4,'yl'=4,'core'=2] {'z','yh'}, dimensions={0} | all-to-all | bytes 18432 | tf_op jit(solution)/shard_map/all_to_all | solution.py:182
  125.2 16.2 %all_to_all.17 = f32[32,2,48]{2,1,0:T(2,128)S(1)} all-to-all(f32[32,2,48]{2,1,0:T(2,128)S(1)} %broadcast_in_dim.2), channel_id=1, replica_groups=mesh['z'=12,'yh'=2,'x'=4,'yl'=4,'core'=2] {'x','yl','core'}, dimensions={0} | all-to-all | bytes 24576 | tf_op jit(solution)/shard_map/all_to_all | solution.py:184
  141.4 0.6 reduce_sum.19
  (3 shorter events, 0.1 us)
Async XLA Ops:
  6.5 96.0 %all-gather.4.cloned.1.call-start = ((), (), s32[]{:S(2)}) async-start(), calls=%async_computation.3 | async-start | bytes 3354624 | tf_op jit(solution)/shard_map/all_gather | solution.py:120
  7.2 0.9 copy-start.3
  20.5 0.9 copy-start.2
  63.2 18.7 %collective-permute-start = (bf16[192,1152]{1,0:T(8,128)(2,1)S(1)}, bf16[192,1152]{1,0:T(8,128)(2,1)S(1)}, u32[]{:S(2)}, u32[]{:S(2)}) collective-permute-start(bf16[192,1152]{1,0:T(8,128)(2,1)S(1)} %all_gather.19._.refs_0_), channel_id=1, source_target_pairs={{0,24},{8,0},{16,8},{24,16},{1,25},{9,1},{17,9},{25,17},{2,26},{10... | collective-permute-start | bytes 1327112 | tf_op jit(solution)/shard_map/ppermute | solution.py:148
  67.5 21.8 %collective-permute-start.3 = (bf16[192,1152]{1,0:T(8,128)(2,1)S(1)}, bf16[192,1152]{1,0:T(8,128)(2,1)S(1)}, u32[]{:S(2)}, u32[]{:S(2)}) collective-permute-start(bf16[192,1152]{1,0:T(8,128)(2,1)S(1)} %all_gather.19._.refs_0_), channel_id=1, source_target_pairs={{0,16},{8,24},{16,0},{24,8},{1,17},{9,25},{17,1},{25,9},{2,18},{10... | collective-permute-start | bytes 1327112 | tf_op jit(solution)/shard_map/ppermute | solution.py:148
  70.0 21.5 %collective-permute-start.5 = (bf16[192,1152]{1,0:T(8,128)(2,1)S(1)}, bf16[192,1152]{1,0:T(8,128)(2,1)S(1)}, u32[]{:S(2)}, u32[]{:S(2)}) collective-permute-start(bf16[192,1152]{1,0:T(8,128)(2,1)S(1)} %all_gather.19._.refs_0_), channel_id=1, source_target_pairs={{0,8},{8,16},{16,24},{24,0},{1,9},{9,17},{17,25},{25,1},{2,10},{10... | collective-permute-start | bytes 1327112 | tf_op jit(solution)/shard_map/ppermute | solution.py:148
  72.5 22.4 %collective-permute-start.1 = (bf16[192,1152]{1,0:T(8,128)(2,1)S(1)}, bf16[192,1152]{1,0:T(8,128)(2,1)S(1)}, u32[]{:S(2)}, u32[]{:S(2)}) collective-permute-start(bf16[192,1152]{1,0:T(8,128)(2,1)S(1)} %all_gather.19._.refs_0_), channel_id=1, source_target_pairs={{0,1},{1,0},{2,3},{3,2},{4,5},{5,4},{6,7},{7,6},{8,9},{9,8},{10,11... | collective-permute-start | bytes 1327112 | tf_op jit(solution)/shard_map/ppermute | solution.py:153
  78.9 2.0 %copy-start = (bf16[1,32,48,1152]{3,2,1,0:T(8,128)(2,1)S(1)}, bf16[1,32,48,1152]{3,2,1,0:T(8,128)(2,1)}, u32[]{:S(2)}) copy-start(bf16[1,32,48,1152]{3,2,1,0:T(8,128)(2,1)} %param.7) | copy-start | bytes 10616836
  81.9 12.9 %collective-permute-start.2 = (bf16[192,1152]{1,0:T(8,128)(2,1)S(1)}, bf16[192,1152]{1,0:T(8,128)(2,1)S(1)}, u32[]{:S(2)}, u32[]{:S(2)}) collective-permute-start(bf16[192,1152]{1,0:T(8,128)(2,1)S(1)} %collective-permute-done.refs_2_), channel_id=1, source_target_pairs={{0,1},{1,0},{2,3},{3,2},{4,5},{5,4},{6,7},{7,6},{8,9},{9,8},{10,11... | collective-permute-start | bytes 1327112 | tf_op jit(solution)/shard_map/ppermute | solution.py:153
  89.3 5.6 %collective-permute-start.4 = (bf16[192,1152]{1,0:T(8,128)(2,1)S(1)}, bf16[192,1152]{1,0:T(8,128)(2,1)S(1)}, u32[]{:S(2)}, u32[]{:S(2)}) collective-permute-start(bf16[192,1152]{1,0:T(8,128)(2,1)S(1)} %collective-permute-done.3.refs_4_), channel_id=1, source_target_pairs={{0,1},{1,0},{2,3},{3,2},{4,5},{5,4},{6,7},{7,6},{8,9},{9,8},{10,11... | collective-permute-start | bytes 1327112 | tf_op jit(solution)/shard_map/ppermute | solution.py:153
  91.5 4.7 %collective-permute-start.6 = (bf16[192,1152]{1,0:T(8,128)(2,1)S(1)}, bf16[192,1152]{1,0:T(8,128)(2,1)S(1)}, u32[]{:S(2)}, u32[]{:S(2)}) collective-permute-start(bf16[192,1152]{1,0:T(8,128)(2,1)S(1)} %collective-permute-done.5.refs_6_), channel_id=1, source_target_pairs={{0,1},{1,0},{2,3},{3,2},{4,5},{5,4},{6,7},{7,6},{8,9},{9,8},{10,11... | collective-permute-start | bytes 1327112 | tf_op jit(solution)/shard_map/ppermute | solution.py:153
  101.0 1.5 %copy-start.1 = (bf16[1152,1152]{1,0:T(8,128)(2,1)}, bf16[1152,1152]{1,0:T(8,128)(2,1)S(1)}, u32[]{:S(2)}) copy-start(bf16[1152,1152]{1,0:T(8,128)(2,1)S(1)} %shard_map.50.proj_ref) | copy-start | bytes 7962628
Sparse Core Ops, SparseCore 0:
  20.0 66.2 all-gather.3

commit v6 on v5

--- a/solution.py
+++ b/solution.py
@@ -23,7 +23,7 @@
     rows = [
         w_ref[(lax.rem(x_ref[0] + step, X) * YL + yl) * CORE + core]
         for step in range(X)
-        for core in (core_ref[0], 1 - core_ref[0])
+        for core in ((core_ref[0], 1 - core_ref[0]) if step < X - 1 else range(CORE))
         for yl in range(YL)
     ]
     out_ref[...] = jnp.concatenate(rows, axis=0).T
@@ -149,8 +149,9 @@
     ]
     further[0], turned = lax.optimization_barrier((further[0], turned))
     blocks = []
-    for block in [rows] + further:
+    for block in [rows] + further[:-1]:
         blocks += [block, lax.ppermute(block, "core", swap)]
+    blocks.append(lax.all_gather(further[-1], "core", axis=0, tiled=True))
 
     proj = pl.pallas_call(
         proj_kernel,

time: 149 us -> 148 us (level)
  blocking collectives: 87.5 us -> 91 us
  starting transfers between devices: 28.2 us -> 24.9 us
    all_gather x0 -> x1, blocking collectives: none -> 3.49 us  [on_device(): blocks.append(lax.all_gather(further[-1], 'core', axis=0, tiled=True))]
    ppermute x4 -> x3, starting transfers between devices: 19 us -> 15.7 us  [on_device(): blocks += [block, lax.ppermute(block, 'core', swap)]]
  transfers between devices with their start and end apart: 8 -> 7, of which waited for: 2 -> 1; matrix products, arithmetic and copies ran while one was open for 0% -> 0% of each run, Pallas kernels for 4% -> 4%
where the time goes in v6:
time: 148 us
  blocking collectives  91 us (61%)
  starting transfers between devices  24.9 us (17%)
  between operations  14.8 us (10%)
  Pallas kernels  10.5 us (7%)
  local copies, waits for them, and re-layouts  5.4 us (4%)
    all_to_all x1, blocking collectives, on_device(): got = lax.all_to_all(pieces, 'z', 0, 0, tiled=True)  23.9 us
    all_to_all x1, blocking collectives, on_device(): lax.all_to_all(part.reshape(Z * YH, share, nb), BAND, 0, 0, tiled=True)  18.3 us
    all_gather x1, blocking collectives, on_device(): rows = lax.all_gather(rows, 'yl', axis=0, tiled=True)  17.5 us
    all_to_all x1, blocking collectives, on_device(): return lax.all_to_all(spread, GA, 0, 0, tiled=True).sum(axis=0)  16.2 us
    ppermute x3, starting transfers between devices, on_device(): blocks += [block, lax.ppermute(block, 'core', swap)]  15.7 us
    all_gather x1, blocking collectives, on_device(): both = lax.optimization_barrier(lax.all_gather(labelled, 'yh'))  11.7 us
    ppermute x3, starting transfers between devices, on_device(): lax.ppermute(rows, 'x', [(i, (i - step) % X) for i in range(X)])  9.21 us
    unnamed x8, local copies, waits for them, and re-layouts  5.39 us
  transfers between devices with their start and end apart: 7, of which 1 were waited for; matrix products, arithmetic and copies ran while one was open for 0% of the time, Pallas kernels for 4%

profile of v6, /device:TPU:1, one launch (start us, length us, event | category | flops | bytes accessed | tf_op | source)
XLA Modules:
  0.0 147.6 jit_solution(7307028494236073570)
XLA Ops:
  6.5 0.0 all-gather.4.cloned.1.call-start
  7.2 0.0 copy-start.3
  7.2 0.9 copy-done.3
  8.1 11.7 %all-gather = bf16[112,1152]{1,0:T(8,128)(2,1)} all-gather(bf16[56,1152]{1,0:T(8,128)(2,1)S(1)} %shard_map.46), channel_id=2, replica_groups=mesh['z'=12,'yh'=2,'x'=4,'yl'=4,'core'=2] {'yh'}, dimensions={0}, use_global_device_ids=true | all-gather | bytes 387072 | tf_op jit(solution)/shard_map/all_gather | solution.py:119
  19.8 0.0 all-gather.4.cloned.1.call-update
  20.5 0.0 copy-start.2
  20.5 0.9 copy-done.2
  21.5 0.3 shard_map.47
  21.7 23.9 %all_to_all.15.got_ref = bf16[12,48,96]{2,1,0:T(8,128)(2,1)S(1)} all-to-all(bf16[12,48,96]{2,1,0:T(8,128)(2,1)S(1)} %shard_map.47), channel_id=1, replica_groups=mesh['z'=12,'yh'=2,'x'=4,'yl'=4,'core'=2] {'z'}, dimensions={0} | all-to-all | bytes 221184 | tf_op jit(solution)/shard_map/all_to_all | solution.py:130
  45.6 0.1 shard_map.48
  45.7 17.5 %all_gather.22._.refs_0_ = bf16[192,1152]{1,0:T(8,128)(2,1)S(1)} all-gather(bf16[48,1152]{1,0:T(8,128)(2,1)S(1)} %shard_map.48), channel_id=1, replica_groups=mesh['z'=12,'yh'=2,'x'=4,'yl'=4,'core'=2] {'yl'}, dimensions={0}, use_global_device_ids=true | all-gather | bytes 552960 | tf_op jit(solution)/shard_map/all_gather | solution.py:138
  63.2 4.3 %collective-permute-start = (bf16[192,1152]{1,0:T(8,128)(2,1)S(1)}, bf16[192,1152]{1,0:T(8,128)(2,1)S(1)}, u32[]{:S(2)}, u32[]{:S(2)}) collective-permute-start(bf16[192,1152]{1,0:T(8,128)(2,1)S(1)} %all_gather.22._.refs_0_), channel_id=1, source_target_pairs={{0,24},{8,0},{16,8},{24,16},{1,25},{9,1},{17,9},{25,17},{2,26},{10... | collective-permute-start | bytes 1327112 | tf_op jit(solution)/shard_map/ppermute | solution.py:148
  67.5 2.5 %collective-permute-start.3 = (bf16[192,1152]{1,0:T(8,128)(2,1)S(1)}, bf16[192,1152]{1,0:T(8,128)(2,1)S(1)}, u32[]{:S(2)}, u32[]{:S(2)}) collective-permute-start(bf16[192,1152]{1,0:T(8,128)(2,1)S(1)} %all_gather.22._.refs_0_), channel_id=1, source_target_pairs={{0,16},{8,24},{16,0},{24,8},{1,17},{9,25},{17,1},{25,9},{2,18},{10... | collective-permute-start | bytes 1327112 | tf_op jit(solution)/shard_map/ppermute | solution.py:148
  70.0 2.4 %collective-permute-start.5 = (bf16[192,1152]{1,0:T(8,128)(2,1)S(1)}, bf16[192,1152]{1,0:T(8,128)(2,1)S(1)}, u32[]{:S(2)}, u32[]{:S(2)}) collective-permute-start(bf16[192,1152]{1,0:T(8,128)(2,1)S(1)} %all_gather.22._.refs_0_), channel_id=1, source_target_pairs={{0,8},{8,16},{16,24},{24,0},{1,9},{9,17},{17,25},{25,1},{2,10},{10... | collective-permute-start | bytes 1327112 | tf_op jit(solution)/shard_map/ppermute | solution.py:148
  72.5 6.5 %collective-permute-start.1 = (bf16[192,1152]{1,0:T(8,128)(2,1)S(1)}, bf16[192,1152]{1,0:T(8,128)(2,1)S(1)}, u32[]{:S(2)}, u32[]{:S(2)}) collective-permute-start(bf16[192,1152]{1,0:T(8,128)(2,1)S(1)} %all_gather.22._.refs_0_), channel_id=1, source_target_pairs={{0,1},{1,0},{2,3},{3,2},{4,5},{5,4},{6,7},{7,6},{8,9},{9,8},{10,11... | collective-permute-start | bytes 1327112 | tf_op jit(solution)/shard_map/ppermute | solution.py:153
  78.9 0.0 copy-start
  78.9 2.0 %copy-done = bf16[1,32,48,1152]{3,2,1,0:T(8,128)(2,1)S(1)} copy-done((bf16[1,32,48,1152]{3,2,1,0:T(8,128)(2,1)S(1)}, bf16[1,32,48,1152]{3,2,1,0:T(8,128)(2,1)}, u32[]{:S(2)}) %copy-start) | copy-done | bytes 3538968
  81.0 1.0 shard_map.49.wt_ref
  81.9 0.0 collective-permute-done.refs_2_
  81.9 7.3 %collective-permute-start.2 = (bf16[192,1152]{1,0:T(8,128)(2,1)S(1)}, bf16[192,1152]{1,0:T(8,128)(2,1)S(1)}, u32[]{:S(2)}, u32[]{:S(2)}) collective-permute-start(bf16[192,1152]{1,0:T(8,128)(2,1)S(1)} %collective-permute-done.refs_2_), channel_id=1, source_target_pairs={{0,1},{1,0},{2,3},{3,2},{4,5},{5,4},{6,7},{7,6},{8,9},{9,8},{10,11... | collective-permute-start | bytes 1327112 | tf_op jit(solution)/shard_map/ppermute | solution.py:153
  89.3 0.0 collective-permute-done.3.refs_4_
  89.3 1.9 %collective-permute-start.4 = (bf16[192,1152]{1,0:T(8,128)(2,1)S(1)}, bf16[192,1152]{1,0:T(8,128)(2,1)S(1)}, u32[]{:S(2)}, u32[]{:S(2)}) collective-permute-start(bf16[192,1152]{1,0:T(8,128)(2,1)S(1)} %collective-permute-done.3.refs_4_), channel_id=1, source_target_pairs={{0,1},{1,0},{2,3},{3,2},{4,5},{5,4},{6,7},{7,6},{8,9},{9,8},{10,11... | collective-permute-start | bytes 1327112 | tf_op jit(solution)/shard_map/ppermute | solution.py:153
  91.2 0.3 collective-permute-done.5
  91.5 3.5 %all_gather.23.refs_6_ = bf16[384,1152]{1,0:T(8,128)(2,1)S(1)} all-gather(bf16[192,1152]{1,0:T(8,128)(2,1)S(1)} %collective-permute-done.5), channel_id=1, replica_groups=mesh['z'=12,'yh'=2,'x'=4,'yl'=4,'core'=2] {'core'}, dimensions={0}, use_global_device_ids=true | all-gather | bytes 1327104 | tf_op jit(solution)/shard_map/all_gather | solution.py:154
  95.0 0.0 collective-permute-done.1.refs_1_
  95.0 0.0 collective-permute-done.2.refs_3_
  95.0 0.0 collective-permute-done.4.refs_5_
  95.0 4.8 %shard_map.50.proj_ref = bf16[1152,1152]{1,0:T(8,128)(2,1)S(1)} custom-call(bf16[1152,1536]{1,0:T(8,128)(2,1)S(1)} %shard_map.49.wt_ref, bf16[192,1152]{1,0:T(8,128)(2,1)S(1)} %all_gather.22._.refs_0_, bf16[192,1152]{1,0:T(8,128)(2,1)S(1)} %collective-permute-done.1.refs_1_, bf16[192,1152]{1,0:T(8,128)(2,1)S(1)} %collective-permute-done.refs_2_, ...), custom_call_target="tpu_custom_call" | custom-call | flops 4076863488 | bytes 10485760 | tf_op jit(solution)/shard_map/pallas_call | solution.py:156
  99.8 0.0 copy-start.1
  99.8 1.5 %copy-done.1 = bf16[1152,1152]{1,0:T(8,128)(2,1)} copy-done((bf16[1152,1152]{1,0:T(8,128)(2,1)}, bf16[1152,1152]{1,0:T(8,128)(2,1)S(1)}, u32[]{:S(2)}) %copy-start.1) | copy-done | bytes 2654232
  101.3 0.0 all-gather.4.cloned.1.call-done
  101.3 4.3 %shard_map.51 = f32[48,48]{1,0:T(8,128)} custom-call(bf16[12,2,56,1152]{3,2,1,0:T(8,128)(2,1)} %bitcast.12, bf16[1152,1152]{1,0:T(8,128)(2,1)} %copy-done.1), custom_call_target="tpu_custom_call" | custom-call | flops 1019215872 | bytes 6291456 | tf_op jit(solution)/shard_map/pallas_call | solution.py:166
  105.7 18.3 %all_to_all.16 = f32[24,2,48]{2,1,0:T(2,128)S(1)} all-to-all(f32[24,2,48]{2,1,0:T(2,128)} %bitcast.13), channel_id=1, replica_groups=mesh['z'=12,'yh'=2,'x'=4,'yl'=4,'core'=2] {'z','yh'}, dimensions={0} | all-to-all | bytes 18432 | tf_op jit(solution)/shard_map/all_to_all | solution.py:183
  124.0 16.2 %all_to_all.17 = f32[32,2,48]{2,1,0:T(2,128)S(1)} all-to-all(f32[32,2,48]{2,1,0:T(2,128)S(1)} %broadcast_in_dim.2), channel_id=1, replica_groups=mesh['z'=12,'yh'=2,'x'=4,'yl'=4,'core'=2] {'x','yl','core'}, dimensions={0} | all-to-all | bytes 24576 | tf_op jit(solution)/shard_map/all_to_all | solution.py:185
  140.2 0.6 reduce_sum.19
  (3 shorter events, 0.1 us)
Async XLA Ops:
  6.5 94.8 %all-gather.4.cloned.1.call-start = ((), (), s32[]{:S(2)}) async-start(), calls=%async_computation.3 | async-start | bytes 3354624 | tf_op jit(solution)/shard_map/all_gather | solution.py:120
  7.2 0.9 copy-start.3
  20.5 0.9 copy-start.2
  63.2 18.7 %collective-permute-start = (bf16[192,1152]{1,0:T(8,128)(2,1)S(1)}, bf16[192,1152]{1,0:T(8,128)(2,1)S(1)}, u32[]{:S(2)}, u32[]{:S(2)}) collective-permute-start(bf16[192,1152]{1,0:T(8,128)(2,1)S(1)} %all_gather.22._.refs_0_), channel_id=1, source_target_pairs={{0,24},{8,0},{16,8},{24,16},{1,25},{9,1},{17,9},{25,17},{2,26},{10... | collective-permute-start | bytes 1327112 | tf_op jit(solution)/shard_map/ppermute | solution.py:148
  67.5 21.8 %collective-permute-start.3 = (bf16[192,1152]{1,0:T(8,128)(2,1)S(1)}, bf16[192,1152]{1,0:T(8,128)(2,1)S(1)}, u32[]{:S(2)}, u32[]{:S(2)}) collective-permute-start(bf16[192,1152]{1,0:T(8,128)(2,1)S(1)} %all_gather.22._.refs_0_), channel_id=1, source_target_pairs={{0,16},{8,24},{16,0},{24,8},{1,17},{9,25},{17,1},{25,9},{2,18},{10... | collective-permute-start | bytes 1327112 | tf_op jit(solution)/shard_map/ppermute | solution.py:148
  70.0 21.5 %collective-permute-start.5 = (bf16[192,1152]{1,0:T(8,128)(2,1)S(1)}, bf16[192,1152]{1,0:T(8,128)(2,1)S(1)}, u32[]{:S(2)}, u32[]{:S(2)}) collective-permute-start(bf16[192,1152]{1,0:T(8,128)(2,1)S(1)} %all_gather.22._.refs_0_), channel_id=1, source_target_pairs={{0,8},{8,16},{16,24},{24,0},{1,9},{9,17},{17,25},{25,1},{2,10},{10... | collective-permute-start | bytes 1327112 | tf_op jit(solution)/shard_map/ppermute | solution.py:148
  72.5 22.6 %collective-permute-start.1 = (bf16[192,1152]{1,0:T(8,128)(2,1)S(1)}, bf16[192,1152]{1,0:T(8,128)(2,1)S(1)}, u32[]{:S(2)}, u32[]{:S(2)}) collective-permute-start(bf16[192,1152]{1,0:T(8,128)(2,1)S(1)} %all_gather.22._.refs_0_), channel_id=1, source_target_pairs={{0,1},{1,0},{2,3},{3,2},{4,5},{5,4},{6,7},{7,6},{8,9},{9,8},{10,11... | collective-permute-start | bytes 1327112 | tf_op jit(solution)/shard_map/ppermute | solution.py:153
  78.9 2.0 %copy-start = (bf16[1,32,48,1152]{3,2,1,0:T(8,128)(2,1)S(1)}, bf16[1,32,48,1152]{3,2,1,0:T(8,128)(2,1)}, u32[]{:S(2)}) copy-start(bf16[1,32,48,1152]{3,2,1,0:T(8,128)(2,1)} %param.7) | copy-start | bytes 10616836
  81.9 13.1 %collective-permute-start.2 = (bf16[192,1152]{1,0:T(8,128)(2,1)S(1)}, bf16[192,1152]{1,0:T(8,128)(2,1)S(1)}, u32[]{:S(2)}, u32[]{:S(2)}) collective-permute-start(bf16[192,1152]{1,0:T(8,128)(2,1)S(1)} %collective-permute-done.refs_2_), channel_id=1, source_target_pairs={{0,1},{1,0},{2,3},{3,2},{4,5},{5,4},{6,7},{7,6},{8,9},{9,8},{10,11... | collective-permute-start | bytes 1327112 | tf_op jit(solution)/shard_map/ppermute | solution.py:153
  89.3 5.7 %collective-permute-start.4 = (bf16[192,1152]{1,0:T(8,128)(2,1)S(1)}, bf16[192,1152]{1,0:T(8,128)(2,1)S(1)}, u32[]{:S(2)}, u32[]{:S(2)}) collective-permute-start(bf16[192,1152]{1,0:T(8,128)(2,1)S(1)} %collective-permute-done.3.refs_4_), channel_id=1, source_target_pairs={{0,1},{1,0},{2,3},{3,2},{4,5},{5,4},{6,7},{7,6},{8,9},{9,8},{10,11... | collective-permute-start | bytes 1327112 | tf_op jit(solution)/shard_map/ppermute | solution.py:153
  99.8 1.5 %copy-start.1 = (bf16[1152,1152]{1,0:T(8,128)(2,1)}, bf16[1152,1152]{1,0:T(8,128)(2,1)S(1)}, u32[]{:S(2)}) copy-start(bf16[1152,1152]{1,0:T(8,128)(2,1)S(1)} %shard_map.50.proj_ref) | copy-start | bytes 7962628
Sparse Core Ops, SparseCore 0:
  20.0 66.2 all-gather.3

commit v7 on v6

--- a/solution.py
+++ b/solution.py
@@ -96,7 +96,11 @@
         )
         for i in range(GROUP):
             sigma += block[i * nb : (i + 1) * nb, i * nb : (i + 1) * nb]
-    out_ref[...] = sigma.T
+    total = sigma.T
+    share = out_ref.shape[1]
+    for place in range(out_ref.shape[0]):
+        start = place // CORE * share
+        out_ref[place] = total[start : start + share]
 
 
 def on_device(pair_dens, energies, freq_index, screened):
@@ -163,9 +167,10 @@
             flops=2 * width * mcols * rowcount, bytes_accessed=10 << 20, transcendentals=0
         ),
     )(turned, *blocks)
+    share = nb // (Z * YH)
     part = pl.pallas_call(
         sigma_kernel,
-        out_shape=jax.ShapeDtypeStruct((nb, nb), jnp.float32),
+        out_shape=jax.ShapeDtypeStruct((Z * YH * CORE, share, nb), jnp.float32),
         in_specs=[pl.BlockSpec(memory_space=pl.ANY)] * 2,
         out_specs=VMEM,
         scratch_shapes=[
@@ -179,10 +184,9 @@
         ),
     )(cols, proj)
 
-    share = nb // (Z * YH)
-    part = lax.all_to_all(part.reshape(Z * YH, share, nb), BAND, 0, 0, tiled=True).sum(axis=0)
-    spread = jnp.broadcast_to(part[None], (X * YL * CORE, share, nb))
-    return lax.all_to_all(spread, GA, 0, 0, tiled=True).sum(axis=0)
+    part = lax.all_to_all(part, BAND + ("core",), 0, 0, tiled=True).sum(axis=0)
+    spread = jnp.broadcast_to(part[None], (X * YL, share, nb))
+    return lax.all_to_all(spread, ("x", "yl"), 0, 0, tiled=True).sum(axis=0)
 
 
 def solution(mesh):

time: 148 us -> 147 us (level)
  no operation moved by 1% of the time
where the time goes in v7:
time: 147 us
  blocking collectives  90.1 us (61%)
  starting transfers between devices  24.9 us (17%)
  between operations  14.8 us (10%)
  Pallas kernels  10.5 us (7%)
  local copies, waits for them, and re-layouts  5.4 us (4%)
    all_to_all x1, blocking collectives, on_device(): got = lax.all_to_all(pieces, 'z', 0, 0, tiled=True)  23.9 us
    all_to_all x1, blocking collectives, on_device(): part = lax.all_to_all(part, BAND + ('core',), 0, 0, tiled=True).sum(axis=0)  20.2 us
    all_gather x1, blocking collectives, on_device(): rows = lax.all_gather(rows, 'yl', axis=0, tiled=True)  17.5 us
    ppermute x3, starting transfers between devices, on_device(): blocks += [block, lax.ppermute(block, 'core', swap)]  15.7 us
    all_to_all x1, blocking collectives, on_device(): return lax.all_to_all(spread, ('x', 'yl'), 0, 0, tiled=True).sum(axis=0)  13.3 us
    all_gather x1, blocking collectives, on_device(): both = lax.optimization_barrier(lax.all_gather(labelled, 'yh'))  11.7 us
    ppermute x3, starting transfers between devices, on_device(): lax.ppermute(rows, 'x', [(i, (i - step) % X) for i in range(X)])  9.21 us
    unnamed x8, local copies, waits for them, and re-layouts  5.39 us
  transfers between devices with their start and end apart: 7, of which 1 were waited for; matrix products, arithmetic and copies ran while one was open for 0% of the time, Pallas kernels for 4%

profile of v7, /device:TPU:1, one launch (start us, length us, event | category | flops | bytes accessed | tf_op | source)
XLA Modules:
  0.0 146.7 jit_solution(5966351074910871014)
XLA Ops:
  6.5 0.0 all-gather.4.cloned.1.call-start
  7.2 0.0 copy-start.3
  7.2 0.9 copy-done.3
  8.1 11.7 %all-gather = bf16[112,1152]{1,0:T(8,128)(2,1)} all-gather(bf16[56,1152]{1,0:T(8,128)(2,1)S(1)} %shard_map.46), channel_id=2, replica_groups=mesh['z'=12,'yh'=2,'x'=4,'yl'=4,'core'=2] {'yh'}, dimensions={0}, use_global_device_ids=true | all-gather | bytes 387072 | tf_op jit(solution)/shard_map/all_gather | solution.py:123
  19.8 0.0 all-gather.4.cloned.1.call-update
  20.5 0.0 copy-start.2
  20.5 0.9 copy-done.2
  21.5 0.3 shard_map.47
  21.7 23.9 %all_to_all.15.got_ref = bf16[12,48,96]{2,1,0:T(8,128)(2,1)S(1)} all-to-all(bf16[12,48,96]{2,1,0:T(8,128)(2,1)S(1)} %shard_map.47), channel_id=1, replica_groups=mesh['z'=12,'yh'=2,'x'=4,'yl'=4,'core'=2] {'z'}, dimensions={0} | all-to-all | bytes 221184 | tf_op jit(solution)/shard_map/all_to_all | solution.py:134
  45.6 0.1 shard_map.48
  45.7 17.5 %all_gather.22._.refs_0_ = bf16[192,1152]{1,0:T(8,128)(2,1)S(1)} all-gather(bf16[48,1152]{1,0:T(8,128)(2,1)S(1)} %shard_map.48), channel_id=1, replica_groups=mesh['z'=12,'yh'=2,'x'=4,'yl'=4,'core'=2] {'yl'}, dimensions={0}, use_global_device_ids=true | all-gather | bytes 552960 | tf_op jit(solution)/shard_map/all_gather | solution.py:142
  63.2 4.3 %collective-permute-start = (bf16[192,1152]{1,0:T(8,128)(2,1)S(1)}, bf16[192,1152]{1,0:T(8,128)(2,1)S(1)}, u32[]{:S(2)}, u32[]{:S(2)}) collective-permute-start(bf16[192,1152]{1,0:T(8,128)(2,1)S(1)} %all_gather.22._.refs_0_), channel_id=1, source_target_pairs={{0,24},{8,0},{16,8},{24,16},{1,25},{9,1},{17,9},{25,17},{2,26},{10... | collective-permute-start | bytes 1327112 | tf_op jit(solution)/shard_map/ppermute | solution.py:152
  67.5 2.5 %collective-permute-start.3 = (bf16[192,1152]{1,0:T(8,128)(2,1)S(1)}, bf16[192,1152]{1,0:T(8,128)(2,1)S(1)}, u32[]{:S(2)}, u32[]{:S(2)}) collective-permute-start(bf16[192,1152]{1,0:T(8,128)(2,1)S(1)} %all_gather.22._.refs_0_), channel_id=1, source_target_pairs={{0,16},{8,24},{16,0},{24,8},{1,17},{9,25},{17,1},{25,9},{2,18},{10... | collective-permute-start | bytes 1327112 | tf_op jit(solution)/shard_map/ppermute | solution.py:152
  70.0 2.4 %collective-permute-start.5 = (bf16[192,1152]{1,0:T(8,128)(2,1)S(1)}, bf16[192,1152]{1,0:T(8,128)(2,1)S(1)}, u32[]{:S(2)}, u32[]{:S(2)}) collective-permute-start(bf16[192,1152]{1,0:T(8,128)(2,1)S(1)} %all_gather.22._.refs_0_), channel_id=1, source_target_pairs={{0,8},{8,16},{16,24},{24,0},{1,9},{9,17},{17,25},{25,1},{2,10},{10... | collective-permute-start | bytes 1327112 | tf_op jit(solution)/shard_map/ppermute | solution.py:152
  72.5 6.5 %collective-permute-start.1 = (bf16[192,1152]{1,0:T(8,128)(2,1)S(1)}, bf16[192,1152]{1,0:T(8,128)(2,1)S(1)}, u32[]{:S(2)}, u32[]{:S(2)}) collective-permute-start(bf16[192,1152]{1,0:T(8,128)(2,1)S(1)} %all_gather.22._.refs_0_), channel_id=1, source_target_pairs={{0,1},{1,0},{2,3},{3,2},{4,5},{5,4},{6,7},{7,6},{8,9},{9,8},{10,11... | collective-permute-start | bytes 1327112 | tf_op jit(solution)/shard_map/ppermute | solution.py:157
  78.9 0.0 copy-start
  78.9 2.0 %copy-done = bf16[1,32,48,1152]{3,2,1,0:T(8,128)(2,1)S(1)} copy-done((bf16[1,32,48,1152]{3,2,1,0:T(8,128)(2,1)S(1)}, bf16[1,32,48,1152]{3,2,1,0:T(8,128)(2,1)}, u32[]{:S(2)}) %copy-start) | copy-done | bytes 3538968
  81.0 1.0 shard_map.49.wt_ref
  81.9 0.0 collective-permute-done.refs_2_
  81.9 7.3 %collective-permute-start.2 = (bf16[192,1152]{1,0:T(8,128)(2,1)S(1)}, bf16[192,1152]{1,0:T(8,128)(2,1)S(1)}, u32[]{:S(2)}, u32[]{:S(2)}) collective-permute-start(bf16[192,1152]{1,0:T(8,128)(2,1)S(1)} %collective-permute-done.refs_2_), channel_id=1, source_target_pairs={{0,1},{1,0},{2,3},{3,2},{4,5},{5,4},{6,7},{7,6},{8,9},{9,8},{10,11... | collective-permute-start | bytes 1327112 | tf_op jit(solution)/shard_map/ppermute | solution.py:157
  89.3 0.0 collective-permute-done.3.refs_4_
  89.3 1.9 %collective-permute-start.4 = (bf16[192,1152]{1,0:T(8,128)(2,1)S(1)}, bf16[192,1152]{1,0:T(8,128)(2,1)S(1)}, u32[]{:S(2)}, u32[]{:S(2)}) collective-permute-start(bf16[192,1152]{1,0:T(8,128)(2,1)S(1)} %collective-permute-done.3.refs_4_), channel_id=1, source_target_pairs={{0,1},{1,0},{2,3},{3,2},{4,5},{5,4},{6,7},{7,6},{8,9},{9,8},{10,11... | collective-permute-start | bytes 1327112 | tf_op jit(solution)/shard_map/ppermute | solution.py:157
  91.2 0.3 collective-permute-done.5
  91.5 3.5 %all_gather.23.refs_6_ = bf16[384,1152]{1,0:T(8,128)(2,1)S(1)} all-gather(bf16[192,1152]{1,0:T(8,128)(2,1)S(1)} %collective-permute-done.5), channel_id=1, replica_groups=mesh['z'=12,'yh'=2,'x'=4,'yl'=4,'core'=2] {'core'}, dimensions={0}, use_global_device_ids=true | all-gather | bytes 1327104 | tf_op jit(solution)/shard_map/all_gather | solution.py:158
  95.0 0.0 collective-permute-done.1.refs_1_
  95.0 0.0 collective-permute-done.2.refs_3_
  95.0 0.0 collective-permute-done.4.refs_5_
  95.0 4.8 %shard_map.50.proj_ref = bf16[1152,1152]{1,0:T(8,128)(2,1)S(1)} custom-call(bf16[1152,1536]{1,0:T(8,128)(2,1)S(1)} %shard_map.49.wt_ref, bf16[192,1152]{1,0:T(8,128)(2,1)S(1)} %all_gather.22._.refs_0_, bf16[192,1152]{1,0:T(8,128)(2,1)S(1)} %collective-permute-done.1.refs_1_, bf16[192,1152]{1,0:T(8,128)(2,1)S(1)} %collective-permute-done.refs_2_, ...), custom_call_target="tpu_custom_call" | custom-call | flops 4076863488 | bytes 10485760 | tf_op jit(solution)/shard_map/pallas_call | solution.py:160
  99.8 0.0 copy-start.1
  99.8 1.5 %copy-done.1 = bf16[1152,1152]{1,0:T(8,128)(2,1)} copy-done((bf16[1152,1152]{1,0:T(8,128)(2,1)}, bf16[1152,1152]{1,0:T(8,128)(2,1)S(1)}, u32[]{:S(2)}) %copy-start.1) | copy-done | bytes 2654232
  101.3 0.0 all-gather.4.cloned.1.call-done
  101.3 4.4 %shard_map.51 = f32[48,2,48]{2,1,0:T(2,128)} custom-call(bf16[12,2,56,1152]{3,2,1,0:T(8,128)(2,1)} %bitcast.11, bf16[1152,1152]{1,0:T(8,128)(2,1)} %copy-done.1), custom_call_target="tpu_custom_call" | custom-call | flops 1019215872 | bytes 6291456 | tf_op jit(solution)/shard_map/pallas_call | solution.py:171
  105.7 20.2 %all_to_all.16 = f32[48,2,48]{2,1,0:T(2,128)S(1)} all-to-all(f32[48,2,48]{2,1,0:T(2,128)} %shard_map.51), channel_id=1, replica_groups=mesh['z'=12,'yh'=2,'x'=4,'yl'=4,'core'=2] {'z','yh','core'}, dimensions={0} | all-to-all | bytes 36864 | tf_op jit(solution)/shard_map/all_to_all | solution.py:187
  125.9 0.1 reduce_sum.18
  126.0 13.3 %all_to_all.17 = f32[16,2,48]{2,1,0:T(2,128)S(1)} all-to-all(f32[16,2,48]{2,1,0:T(2,128)S(1)} %broadcast_in_dim.2), channel_id=1, replica_groups=mesh['z'=12,'yh'=2,'x'=4,'yl'=4,'core'=2] {'x','yl'}, dimensions={0} | all-to-all | bytes 12288 | tf_op jit(solution)/shard_map/all_to_all | solution.py:189
  139.3 0.6 reduce_sum.19
  (2 shorter events, 0.0 us)
Async XLA Ops:
  6.5 94.8 %all-gather.4.cloned.1.call-start = ((), (), s32[]{:S(2)}) async-start(), calls=%async_computation.3 | async-start | bytes 3354624 | tf_op jit(solution)/shard_map/all_gather | solution.py:124
  7.2 0.9 copy-start.3
  20.5 0.9 copy-start.2
  63.2 18.7 %collective-permute-start = (bf16[192,1152]{1,0:T(8,128)(2,1)S(1)}, bf16[192,1152]{1,0:T(8,128)(2,1)S(1)}, u32[]{:S(2)}, u32[]{:S(2)}) collective-permute-start(bf16[192,1152]{1,0:T(8,128)(2,1)S(1)} %all_gather.22._.refs_0_), channel_id=1, source_target_pairs={{0,24},{8,0},{16,8},{24,16},{1,25},{9,1},{17,9},{25,17},{2,26},{10... | collective-permute-start | bytes 1327112 | tf_op jit(solution)/shard_map/ppermute | solution.py:152
  67.5 21.8 %collective-permute-start.3 = (bf16[192,1152]{1,0:T(8,128)(2,1)S(1)}, bf16[192,1152]{1,0:T(8,128)(2,1)S(1)}, u32[]{:S(2)}, u32[]{:S(2)}) collective-permute-start(bf16[192,1152]{1,0:T(8,128)(2,1)S(1)} %all_gather.22._.refs_0_), channel_id=1, source_target_pairs={{0,16},{8,24},{16,0},{24,8},{1,17},{9,25},{17,1},{25,9},{2,18},{10... | collective-permute-start | bytes 1327112 | tf_op jit(solution)/shard_map/ppermute | solution.py:152
  70.0 21.5 %collective-permute-start.5 = (bf16[192,1152]{1,0:T(8,128)(2,1)S(1)}, bf16[192,1152]{1,0:T(8,128)(2,1)S(1)}, u32[]{:S(2)}, u32[]{:S(2)}) collective-permute-start(bf16[192,1152]{1,0:T(8,128)(2,1)S(1)} %all_gather.22._.refs_0_), channel_id=1, source_target_pairs={{0,8},{8,16},{16,24},{24,0},{1,9},{9,17},{17,25},{25,1},{2,10},{10... | collective-permute-start | bytes 1327112 | tf_op jit(solution)/shard_map/ppermute | solution.py:152
  72.5 22.6 %collective-permute-start.1 = (bf16[192,1152]{1,0:T(8,128)(2,1)S(1)}, bf16[192,1152]{1,0:T(8,128)(2,1)S(1)}, u32[]{:S(2)}, u32[]{:S(2)}) collective-permute-start(bf16[192,1152]{1,0:T(8,128)(2,1)S(1)} %all_gather.22._.refs_0_), channel_id=1, source_target_pairs={{0,1},{1,0},{2,3},{3,2},{4,5},{5,4},{6,7},{7,6},{8,9},{9,8},{10,11... | collective-permute-start | bytes 1327112 | tf_op jit(solution)/shard_map/ppermute | solution.py:157
  78.9 2.0 %copy-start = (bf16[1,32,48,1152]{3,2,1,0:T(8,128)(2,1)S(1)}, bf16[1,32,48,1152]{3,2,1,0:T(8,128)(2,1)}, u32[]{:S(2)}) copy-start(bf16[1,32,48,1152]{3,2,1,0:T(8,128)(2,1)} %param.7) | copy-start | bytes 10616836
  81.9 13.1 %collective-permute-start.2 = (bf16[192,1152]{1,0:T(8,128)(2,1)S(1)}, bf16[192,1152]{1,0:T(8,128)(2,1)S(1)}, u32[]{:S(2)}, u32[]{:S(2)}) collective-permute-start(bf16[192,1152]{1,0:T(8,128)(2,1)S(1)} %collective-permute-done.refs_2_), channel_id=1, source_target_pairs={{0,1},{1,0},{2,3},{3,2},{4,5},{5,4},{6,7},{7,6},{8,9},{9,8},{10,11... | collective-permute-start | bytes 1327112 | tf_op jit(solution)/shard_map/ppermute | solution.py:157
  89.3 5.7 %collective-permute-start.4 = (bf16[192,1152]{1,0:T(8,128)(2,1)S(1)}, bf16[192,1152]{1,0:T(8,128)(2,1)S(1)}, u32[]{:S(2)}, u32[]{:S(2)}) collective-permute-start(bf16[192,1152]{1,0:T(8,128)(2,1)S(1)} %collective-permute-done.3.refs_4_), channel_id=1, source_target_pairs={{0,1},{1,0},{2,3},{3,2},{4,5},{5,4},{6,7},{7,6},{8,9},{9,8},{10,11... | collective-permute-start | bytes 1327112 | tf_op jit(solution)/shard_map/ppermute | solution.py:157
  99.8 1.5 %copy-start.1 = (bf16[1152,1152]{1,0:T(8,128)(2,1)}, bf16[1152,1152]{1,0:T(8,128)(2,1)S(1)}, u32[]{:S(2)}) copy-start(bf16[1152,1152]{1,0:T(8,128)(2,1)S(1)} %shard_map.50.proj_ref) | copy-start | bytes 7962628
Sparse Core Ops, SparseCore 0:
  20.0 66.2 all-gather.3
